TPU v7x, 128 devices: a whole 4x4x4 slice. The times are simulated.
128 devices in a mesh: phi: 8 (over y, core), eta: 16 (over x, z).
Axes of the slice: x: 4, y: 4, z: 4, core: 2. Of those that a mesh axis runs over, the one named last changes fastest.
Arguments:
- edges: bfloat16 [262144, 128], P(('phi', 'eta')), may hold values from -6 to 6
- cotangent: bfloat16 [262144, 128], P(('phi', 'eta')), may hold values from -6 to 6
- send_rows: int32 [128, 128, 32], P(('phi', 'eta')), may hold values from 0 to 2047
- send_count: int32 [128, 128], P(('phi', 'eta')), may hold values from 1 to 32, as said below
- trip_local: int32 [1048576], P(('phi', 'eta')), may hold values from 0 to 2047
- trip_remote: int32 [1048576], P(('phi', 'eta')), may hold values from 0 to 4095, as said below
- w_first: bfloat16 [384, 256], replicated, may hold values from -0.3125 to 0.3125
- bias_first: float32 [256], replicated, may hold values from -4 to 4
- w_second: bfloat16 [256, 128], replicated, may hold values from -0.375 to 0.375
Outputs:
- new_edges: bfloat16 [262144, 128], P(('phi', 'eta'))
- edge_grad: bfloat16 [262144, 128], P(('phi', 'eta'))
- grad_first: float32 [384, 256], replicated
- grad_bias: float32 [256], replicated
- grad_second: float32 [256, 128], replicated
Inputs may be any that keep to these rules, and one draw needn't show every extreme that they name: `send_count`: some destination device has every slot live from every source. `trip_remote`: each triplet names a live slot of a source device toward its own owner.
All inputs are finite; a program needn't handle non-finite values.
Results may differ from a plain program's by a relative error of at most 0.0053.
Values may be sent and summed in bfloat16 or wider, within the bound.
No kernel may reach another device: no remote copies, remote signals or barrier semaphores. Data moves between devices by JAX's collectives and lax.ppermute only.
A program may use at most 128 MiB of HBM per device.

v0:
```python
import jax
import jax.numpy as jnp
from jax import lax
from jax.sharding import PartitionSpec as P


def silu_slope(pre):
    sig = jax.nn.sigmoid(pre)
    return sig * (1.0 + pre * (1.0 - sig))


def local(
    edges, cotangent, send_rows, send_count, trip_local, trip_remote, w_first, bias_first, w_second
):
    width = edges.shape[1]
    local_edges = edges.shape[0]
    n_phi = lax.axis_size("phi")
    n_eta = lax.axis_size("eta")
    ndev = n_phi * n_eta
    slots_per = send_rows.shape[2]
    rows = send_rows[0]
    live = jnp.arange(slots_per, dtype=jnp.int32)[None, :] < send_count[0][:, None]
    zero = jnp.zeros((), jnp.bfloat16)
    stacked = jnp.stack([edges, cotangent], axis=1)
    outgoing = jnp.where(live[:, :, None, None], stacked[rows], zero)
    arrived = lax.all_to_all(outgoing, ("phi", "eta"), split_axis=0, concat_axis=0, tiled=True)
    arrived = arrived.reshape(ndev * slots_per, 2, width)
    inner = edges[trip_local]
    inner_cot = cotangent[trip_local]
    outer_pair = arrived[trip_remote]
    outer = outer_pair[:, 0, :]
    outer_cot = outer_pair[:, 1, :]
    inner_f = inner.astype(jnp.float32)
    outer_f = outer.astype(jnp.float32)
    prod = (inner_f * outer_f).astype(jnp.bfloat16)
    joined = jnp.concatenate([inner, outer, prod], axis=1)
    pre = jnp.dot(joined, w_first, preferred_element_type=jnp.float32) + bias_first
    hidden = jax.nn.silu(pre).astype(jnp.bfloat16)
    message = jnp.dot(hidden, w_second, preferred_element_type=jnp.float32)
    dmsg = (inner_cot.astype(jnp.float32) + outer_cot.astype(jnp.float32)).astype(jnp.bfloat16)
    dpre = jnp.dot(dmsg, w_second.T, preferred_element_type=jnp.float32) * silu_slope(pre)
    dpre_b = dpre.astype(jnp.bfloat16)
    dx = jnp.dot(dpre_b, w_first.T, preferred_element_type=jnp.float32)
    d_inner = dx[:, :width] + dx[:, 2 * width :] * outer_f
    d_outer = dx[:, width : 2 * width] + dx[:, 2 * width :] * inner_f
    slot_msg = jax.ops.segment_sum(message, trip_remote, ndev * slots_per)
    slot_grad = jax.ops.segment_sum(d_outer, trip_remote, ndev * slots_per)
    slot_sums = (
        jnp.stack([slot_msg, slot_grad], axis=1)
        .astype(jnp.bfloat16)
        .reshape(ndev, slots_per, 2, width)
    )
    returned = lax.all_to_all(slot_sums, ("phi", "eta"), split_axis=0, concat_axis=0, tiled=True)
    returned = jnp.where(live[:, :, None, None], returned, zero)
    grad_second = jnp.dot(hidden.T, dmsg, preferred_element_type=jnp.float32)
    grad_first = jnp.dot(joined.T, dpre_b, preferred_element_type=jnp.float32)
    grad_bias = jnp.sum(dpre, axis=0)
    grad_first, grad_bias, grad_second = lax.psum(
        (grad_first, grad_bias, grad_second), ("phi", "eta")
    )
    local_msg = jax.ops.segment_sum(message, trip_local, local_edges)
    local_grad = jax.ops.segment_sum(d_inner, trip_local, local_edges)
    flat_rows = rows.reshape(-1)
    local_msg = local_msg.at[flat_rows].add(
        returned[:, :, 0, :].astype(jnp.float32).reshape(-1, width)
    )
    local_grad = local_grad.at[flat_rows].add(
        returned[:, :, 1, :].astype(jnp.float32).reshape(-1, width)
    )
    new_edges = (edges.astype(jnp.float32) + local_msg).astype(jnp.bfloat16)
    edge_grad = (cotangent.astype(jnp.float32) + local_grad).astype(jnp.bfloat16)
    return (new_edges, edge_grad, grad_first, grad_bias, grad_second)


def solution(mesh):
    in_specs = (
        P(("phi", "eta"), None),
        P(("phi", "eta"), None),
        P(("phi", "eta"), None, None),
        P(("phi", "eta"), None),
        P(("phi", "eta")),
        P(("phi", "eta")),
        P(),
        P(),
        P(),
    )
    out_specs = (P(("phi", "eta"), None), P(("phi", "eta"), None), P(), P(), P())
    return jax.shard_map(local, mesh=mesh, in_specs=in_specs, out_specs=out_specs, check_vma=False)
```

profile of v0, /device:TPU:1, one launch (start us, length us, event | category | flops | bytes accessed | tf_op | source)
XLA Modules:
  0.0 576.2 jit_solution(11426100042497210665)
XLA Ops:
  14.9 26.9 %gather_fusion.1 = bf16[4096,2,128]{2,1,0:T(2,128)(2,1)} fusion(bf16[2048,2,128]{2,1,0:T(2,128)(2,1)S(1)} %pad_maximum_fusion.4, s32[4096]{0:T(1024)S(1)} %broadcast_clamp_fusion), kind=kCustom, calls=%fused_computation.1 | custom fusion | bytes 4210688 | tf_op jit(solution)/shard_map/gather | solution.py:25
  41.9 3.2 copy_select_fusion
  45.1 12.0 %all-to-all-start = ((bf16[128,32,2,128]{3,1,2,0:T(8,128)(2,1)}), bf16[128,32,2,128]{3,1,2,0:T(8,128)(2,1)}, u32[]{:S(2)}, u32[]{:S(2)}) async-start(bf16[128,32,2,128]{3,1,2,0:T(8,128)(2,1)} %copy_select_fusion), calls=%async_computation | async-start | bytes 4194304 | tf_op jit(solution)/shard_map/all_to_all | solution.py:26
  58.4 29.2 %gather_fusion = bf16[8192,128]{1,0:T(8,128)(2,1)} fusion(bf16[2048,128]{1,0:T(8,128)(2,1)S(1)} %copy-done.2, s32[8192]{0:T(1024)S(1)} %fusion.22), kind=kCustom, calls=%fused_computation | custom fusion | bytes 4227072 | tf_op jit(solution)/shard_map/gather | solution.py:28
  87.6 29.2 %gather_fusion.3 = bf16[8192,128]{1,0:T(8,128)(2,1)} fusion(bf16[2048,128]{1,0:T(8,128)(2,1)S(1)} %copy-done.3, s32[8192]{0:T(1024)S(1)} %fusion.22), kind=kCustom, calls=%fused_computation.3 | custom fusion | bytes 4227072 | tf_op jit(solution)/shard_map/gather | solution.py:29
  116.9 4.0 copy.28
  120.9 53.3 %gather_fusion.2 = bf16[8192,2,128]{2,1,0:T(2,128)(2,1)} fusion(bf16[4096,2,128]{2,1,0:T(2,128)(2,1)S(1)} %bitcast.30, s32[8192]{0:T(1024)S(1)} %fusion.23), kind=kCustom, calls=%fused_computation.2 | custom fusion | bytes 8421376 | tf_op jit(solution)/shard_map/gather | solution.py:30
  174.3 9.6 %slice_convert_fusion = (f32[8192,1,128]{2,1,0:T(1,128)}, bf16[8192,1,128]{2,1,0:T(2,128)(2,1)S(1)}) fusion(bf16[8192,2,128]{2,1,0:T(2,128)(2,1)} %gather_fusion.2), kind=kLoop, calls=%fused_computation.25 | loop fusion | flops 1048576 | bytes 10485760 | tf_op jit(solution)/shard_map/convert_element_type | solution.py:40
  184.8 5.2 multiply_convert_fusion
  191.9 3.2 fusion.29
  195.1 45.8 %scatter_custom_fusion.1 = f32[4096,128]{1,0:T(8,128)} fusion(s32[8192]{0:T(1024)S(1)} %copy-done.16, f32[8192,128]{1,0:T(8,128)} %fusion.29, f32[]{:T(128)} %constant.11.clone.1), kind=kCustom, calls=%fused_computation.43 | custom fusion | flops 1048576 | bytes 2097664 | tf_op jit(solution)/shard_map/scatter-add | solution.py:46
  240.9 2.7 convert.11
  243.5 7.9 %fusion.28 = (f32[256]{0:T(256)S(1)}, bf16[8192,256]{1,0:T(8,128)(2,1)S(1)}) fusion(f32[8192,256]{1,0:T(8,128)} %get-tuple-element.14, bf16[256,128]{1,0:T(8,128)(2,1)S(1)} %copy-done.14, f32[8192,128]{1,0:T(8,128)} %bitcast.31, bf16[8192,128]{1,0:T(8,128)(2,1)} %gather_fusion.3), kind=kOutput, calls=%fused_computation.57 | convolution fusion | flops 560987904 | bytes 18940928 | tf_op jit(solution)/shard_map/dot_general | solution.py:41
  253.4 6.9 %fusion.17 = f32[8192,384]{1,0:T(8,128)} fusion(bf16[384,256]{1,0:T(8,128)(2,1)S(1)} %copy-done, bf16[8192,256]{1,0:T(8,128)(2,1)S(1)} %get-tuple-element.16), kind=kOutput, calls=%fused_computation.38 | convolution fusion | flops 1610612736 | bytes 16973824 | tf_op jit(solution)/shard_map/dot_general | solution.py:43
  260.4 46.4 %scatter_custom_fusion.2 = f32[4096,128]{1,0:T(8,128)} fusion(s32[8192]{0:T(1024)S(1)} %copy-done.16, bf16[8192,128]{1,0:T(8,128)(2,1)S(1)} %copy-done.5, f32[8192,384]{1,0:T(8,128)} %fusion.17, f32[]{:T(128)} %constant.11.clone.1), kind=kCustom, calls=%fused_computation.19 | custom fusion | flops 4194304 | bytes 12583424 | tf_op jit(solution)/shard_map/scatter-add | solution.py:47
  311.9 10.2 %all-to-all-start.1 = ((bf16[128,32,2,128]{3,1,2,0:T(8,128)(2,1)}), bf16[128,32,2,128]{3,1,2,0:T(8,128)(2,1)}, u32[]{:S(2)}, u32[]{:S(2)}) async-start(bf16[128,32,2,128]{3,1,2,0:T(8,128)(2,1)} %copy.31), calls=%async_computation.1 | async-start | bytes 4194304 | tf_op jit(solution)/shard_map/all_to_all | solution.py:53
  322.2 44.7 %scatter_fusion = f32[2048,128]{1,0:T(8,128)S(1)} fusion(f32[2048,128]{1,0:T(8,128)S(1)} %convert_element_type.55, s32[8192]{0:T(1024)S(1)} %copy-done.13, f32[8192,128]{1,0:T(8,128)} %fusion.29), kind=kCustom, calls=%fused_computation.4 | custom fusion | flops 1048576 | bytes 12615680 | tf_op jit(solution)/shard_map/scatter-add | solution.py:61
  367.0 42.8 %scatter_custom_fusion.4 = f32[2048,128]{1,0:T(8,128)} fusion(f32[2048,128]{1,0:T(8,128)} %convert_element_type.68, s32[8192]{0:T(1024)S(1)} %copy-done.13, bf16[8192,128]{1,0:T(8,128)(2,1)} %copy-done.6, f32[8192,384]{1,0:T(8,128)} %fusion.17), kind=kCustom, calls=%fused_computation.22 | custom fusion | flops 4194304 | bytes 11534336 | tf_op jit(solution)/shard_map/scatter-add | solution.py:62
  409.8 6.1 %fusion.26 = f32[256,128]{1,0:T(8,128)} fusion(bf16[8192,256]{1,0:T(8,128)(2,1)} %copy-done.4, f32[8192,128]{1,0:T(8,128)} %bitcast.32, bf16[8192,128]{1,0:T(8,128)(2,1)} %gather_fusion.3), kind=kOutput, calls=%fused_computation.55 | convolution fusion | flops 540016640 | bytes 10616832 | tf_op jit(solution)/shard_map/dot_general | solution.py:55
  416.3 2.6 fusion.11
  418.9 67.5 %psum.22 = f32[256]{0:T(256)} all-reduce(f32[256]{0:T(256)S(1)} %get-tuple-element.15), channel_id=1, replica_groups=mesh['phi'=8,'eta'=16] {'phi','eta'}, use_global_device_ids=true, to_apply=%region_8.9 | all-reduce | flops 256 | bytes 2048 | tf_op jit(solution)/shard_map/psum | solution.py:58
  489.7 23.2 %scatter_custom_fusion.5 = f32[2048,128]{1,0:T(8,128)S(1)} fusion(f32[2048,128]{1,0:T(8,128)S(1)} %copy-done.10, s32[4096]{0:T(1024)S(1)} %bitcast.38, bf16[4096,128]{1,0:T(8,128)(2,1)} %bitcast.37), kind=kCustom, calls=%fused_computation.32 | custom fusion | flops 1048576 | bytes 2097152 | tf_op jit(solution)/shard_map/scatter-add | solution.py:67
  513.8 22.8 %scatter_custom_fusion.3 = f32[2048,128]{1,0:T(8,128)S(1)} fusion(f32[2048,128]{1,0:T(8,128)S(1)} %scatter_fusion, s32[4096]{0:T(1024)S(1)} %bitcast.39, bf16[4096,128]{1,0:T(8,128)(2,1)S(1)} %bitcast.36), kind=kCustom, calls=%fused_computation.34 | custom fusion | flops 1048576 | bytes 2097152 | tf_op jit(solution)/shard_map/scatter-add | solution.py:64
  537.4 28.6 %all-reduce.3.cloned.1.call-done = (f32[384,256]{1,0:T(8,128)}, f32[256,128]{1,0:T(8,128)}) async-done(((f32[384,256]{1,0:T(8,128)}, f32[256,128]{1,0:T(8,128)}), (f32[384,256]{1,0:T(8,128)}, f32[256,128]{1,0:T(8,128)})) %all-reduce.3.cloned.1.call-update) | async-done | bytes 524304 | tf_op jit(solution)/shard_map/psum | solution.py:58
  (65 shorter events, 27.8 us)
Async XLA Ops:
  7.2 177.6 %copy-start = (bf16[384,256]{1,0:T(8,128)(2,1)S(1)}, bf16[384,256]{1,0:T(8,128)(2,1)}, u32[]{:S(2)}) copy-start(bf16[384,256]{1,0:T(8,128)(2,1)} %param.15) | copy-start | bytes 589828
  41.9 15.2 %copy-start.15 = (s32[1,128,32]{1,2,0:T(8,128)S(1)}, s32[1,128,32]{1,2,0:T(8,128)}, u32[]{:S(2)}) copy-start(s32[1,128,32]{1,2,0:T(8,128)} %param.11) | copy-start | bytes 49156
  41.9 15.3 %copy-start.2 = (bf16[2048,128]{1,0:T(8,128)(2,1)S(1)}, bf16[2048,128]{1,0:T(8,128)(2,1)}, u32[]{:S(2)}) copy-start(bf16[2048,128]{1,0:T(8,128)(2,1)} %param.9) | copy-start | bytes 1572868
  41.9 15.4 %copy-start.3 = (bf16[2048,128]{1,0:T(8,128)(2,1)S(1)}, bf16[2048,128]{1,0:T(8,128)(2,1)}, u32[]{:S(2)}) copy-start(bf16[2048,128]{1,0:T(8,128)(2,1)} %param.10) | copy-start | bytes 1572868
  45.1 13.3 %copy-start.13 = (s32[8192]{0:T(1024)S(1)}, s32[8192]{0:T(1024)}, u32[]{:S(2)}) copy-start(s32[8192]{0:T(1024)} %param.13) | copy-start | bytes 98308
  45.1 71.8 %all-to-all-start = ((bf16[128,32,2,128]{3,1,2,0:T(8,128)(2,1)}), bf16[128,32,2,128]{3,1,2,0:T(8,128)(2,1)}, u32[]{:S(2)}, u32[]{:S(2)}) async-start(bf16[128,32,2,128]{3,1,2,0:T(8,128)(2,1)} %copy_select_fusion), calls=%async_computation | async-start | bytes 4194304 | tf_op jit(solution)/shard_map/all_to_all | solution.py:26
  87.6 29.3 %copy-start.16 = (s32[8192]{0:T(1024)S(1)}, s32[8192]{0:T(1024)}, u32[]{:S(2)}) copy-start(s32[8192]{0:T(1024)} %param.14) | copy-start | bytes 98308
  174.3 9.6 %copy-start.5 = (bf16[8192,128]{1,0:T(8,128)(2,1)S(1)}, bf16[8192,128]{1,0:T(8,128)(2,1)}, u32[]{:S(2)}) copy-start(bf16[8192,128]{1,0:T(8,128)(2,1)} %gather_fusion) | copy-start | bytes 6291460
  183.9 0.9 copy-start.17
  184.7 5.3 copy-start.6
  184.7 5.3 copy-start.11
  184.7 7.2 %copy-start.14 = (bf16[256,128]{1,0:T(8,128)(2,1)S(1)}, bf16[256,128]{1,0:T(8,128)(2,1)}, u32[]{:S(2)}) copy-start(bf16[256,128]{1,0:T(8,128)(2,1)} %param.17) | copy-start | bytes 196612
  190.0 1.9 copy-start.4
  251.5 2.0 copy-start.8
  311.9 174.4 %all-to-all-start.1 = ((bf16[128,32,2,128]{3,1,2,0:T(8,128)(2,1)}), bf16[128,32,2,128]{3,1,2,0:T(8,128)(2,1)}, u32[]{:S(2)}, u32[]{:S(2)}) async-start(bf16[128,32,2,128]{3,1,2,0:T(8,128)(2,1)} %copy.31), calls=%async_computation.1 | async-start | bytes 4194304 | tf_op jit(solution)/shard_map/all_to_all | solution.py:53
  322.2 243.8 %all-reduce.3.cloned.1.call-start = ((), (), s32[]{:S(2)}) async-start(), calls=%async_computation.2 | async-start | bytes 1048576 | tf_op jit(solution)/shard_map/psum | solution.py:58
  409.8 6.2 %copy-start.7 = (bf16[8192,128]{1,0:T(8,128)(2,1)S(1)}, bf16[8192,128]{1,0:T(8,128)(2,1)}, u32[]{:S(2)}) copy-start(bf16[8192,128]{1,0:T(8,128)(2,1)} %copy-done.6) | copy-start | bytes 6291460
  409.8 6.2 %copy-start.9 = (bf16[8192,256]{1,0:T(8,128)(2,1)S(1)}, bf16[8192,256]{1,0:T(8,128)(2,1)}, u32[]{:S(2)}) copy-start(bf16[8192,256]{1,0:T(8,128)(2,1)} %copy-done.8) | copy-start | bytes 12582916
  409.8 6.5 %copy-start.12 = (bf16[8192,128]{1,0:T(8,128)(2,1)S(1)}, bf16[8192,128]{1,0:T(8,128)(2,1)}, u32[]{:S(2)}) copy-start(bf16[8192,128]{1,0:T(8,128)(2,1)} %copy-done.11) | copy-start | bytes 6291460
  486.3 3.4 copy-start.10
  489.7 79.6 %copy-start.1 = (bf16[384,256]{1,0:T(8,128)(2,1)S(1)}, bf16[384,256]{1,0:T(8,128)(2,1)}, u32[]{:S(2)}) copy-start(bf16[384,256]{1,0:T(8,128)(2,1)} %param.15) | copy-start | bytes 589828
Sparse Core Ops, SparseCore 0:
  419.0 146.9 all-reduce.2
where the time goes:
time: 577 us; the launch traced here: 576 us
  other arithmetic  254 us (44%)
  local copies, waits for them, and re-layouts  158 us (27%)
  blocking collectives  67.5 us (12%)
  matrix products  32 us (6%)
  waiting for transfers between devices  28.6 us (5%)
  starting transfers between devices  22.2 us (4%)
  between operations  14.3 us (2%)
    psum x1, blocking collectives, local(): lax.psum((grad_first, grad_bias, grad_second), ('phi', 'eta'))  67.5 us
    gather x1, local copies, waits for them, and re-layouts, local(): outer_pair = arrived[trip_remote]  53.3 us
    scatter-add x1, other arithmetic, local(): slot_grad = jax.ops.segment_sum(d_outer, trip_remote, ndev * slots_per)  46.4 us
    scatter-add x1, other arithmetic, local(): slot_msg = jax.ops.segment_sum(message, trip_remote, ndev * slots_per)  45.8 us
    scatter-add x1, other arithmetic, local(): local_msg = jax.ops.segment_sum(message, trip_local, local_edges)  44.7 us
    scatter-add x1, other arithmetic, local(): local_grad = jax.ops.segment_sum(d_inner, trip_local, local_edges)  42.8 us
    gather x1, local copies, waits for them, and re-layouts, local(): inner_cot = cotangent[trip_local]  29.2 us
    gather x1, local copies, waits for them, and re-layouts, local(): inner = edges[trip_local]  29.2 us
  transfers between devices with their start and end apart: 3, of which 1 were waited for; matrix products, arithmetic and copies ran while one was open for 36% of the time, Pallas kernels for 0%

commit v1 on v0

v1 whole, which is shorter than its diff:
```python
import functools

import jax
import jax.numpy as jnp
from jax import lax
from jax.experimental import pallas as pl
from jax.experimental.pallas import tpu as pltpu
from jax.sharding import PartitionSpec as P

AXES = ("phi", "eta")
BLOCK = 256
WINDOW = 256
BF16 = jnp.bfloat16
F32 = jnp.float32


def dot(a, b):
    return jnp.dot(a, b, preferred_element_type=F32)


def dot_rows(a, b):
    return lax.dot_general(a, b, (((0,), (0,)), ((), ())), preferred_element_type=F32)


def triplet_kernel(
    slots,
    base_ref,
    count_ref,
    col_ref,
    row_ref,
    own_ref,
    far_ref,
    w1_ref,
    w1t_ref,
    w2_ref,
    w2t_ref,
    bias_ref,
    inner_ref,
    slot_ref,
    grad_ref,
    gbias_ref,
    total_ref,
    part_ref,
):
    width = own_ref.shape[1] // 2
    step = pl.program_id(0)

    @pl.when(step == 0)
    def _():
        total_ref[...] = jnp.zeros_like(total_ref)
        grad_ref[...] = jnp.zeros_like(grad_ref)
        gbias_ref[...] = jnp.zeros_like(gbias_ref)

    base = base_ref[step]
    count = count_ref[step]

    def window(w):
        first = base + w * WINDOW
        return first, pl.multiple_of(jnp.minimum(first, slots - WINDOW), 16)

    def pick(w):
        first, start = window(w)
        col = col_ref[...]
        rel = jnp.where(col >= first, col - start, -1)
        lane = lax.broadcasted_iota(jnp.int32, rel.shape, 1)
        hot = jnp.concatenate(
            [(rel == lane + k * 128).astype(F32).astype(BF16) for k in range(WINDOW // 128)], axis=1
        )
        return dot(hot, far_ref[pl.ds(start, WINDOW), :])

    part_ref[...] = pick(0)

    @pl.when(count > 1)
    def _():
        def more(w, carry):
            part_ref[...] += pick(w)
            return carry

        lax.fori_loop(1, count, more, 0)

    far = part_ref[...]
    b = far[:, :width]
    gb = far[:, width:]
    own = own_ref[...]
    a = own[:, :width]
    ga = own[:, width:]
    af = a.astype(F32)
    prod = (af * b).astype(BF16)
    x = jnp.concatenate([a, b.astype(BF16), prod], axis=1)
    pre = dot(x, w1_ref[...]) + bias_ref[...]
    sig = jax.nn.sigmoid(pre)
    h = (pre * sig).astype(BF16)
    m = dot(h, w2_ref[...])
    dm = (ga.astype(F32) + gb).astype(BF16)
    dpre = dot(dm, w2t_ref[...]) * (sig * (1.0 + pre * (1.0 - sig)))
    dpre_b = dpre.astype(BF16)
    dx = dot(dpre_b, w1t_ref[...])
    dprod = dx[:, 2 * width :]
    da = dx[:, :width] + dprod * b
    db = dx[:, width : 2 * width] + dprod * af
    mb = m.astype(BF16)
    inner_ref[...] = jnp.concatenate([mb, da.astype(BF16)], axis=1)
    outer = jnp.concatenate([mb, db.astype(BF16)], axis=1)
    rows1 = x.shape[1]
    grad_ref[:rows1, :] += dot_rows(x, dpre_b)
    grad_ref[rows1:, :] += dot_rows(dm, h)
    gbias_ref[...] += jnp.sum(dpre, axis=0, keepdims=True)

    def put(w):
        first, start = window(w)
        row = row_ref[0]
        rel = jnp.where(row >= first, row - start, -1)
        at = lax.broadcasted_iota(jnp.int32, (WINDOW, row.shape[1]), 0)
        hot = (at == rel).astype(F32).astype(BF16)
        total_ref[pl.ds(start, WINDOW), :] += dot(hot, outer)

    put(0)

    @pl.when(count > 1)
    def _():
        def more(w, carry):
            put(w)
            return carry

        lax.fori_loop(1, count, more, 0)

    @pl.when(step == pl.num_programs(0) - 1)
    def _():
        slot_ref[...] = total_ref[...].astype(BF16)


def triplets(remote, own, far, w1, bias, w2):
    trips = remote.shape[0]
    slots, pair = far.shape
    width = pair // 2
    hid = w1.shape[1]
    rows1 = w1.shape[0]
    steps = trips // BLOCK
    blocks = remote.reshape(steps, BLOCK)
    base = jnp.minimum(blocks[:, 0] // 16 * 16, slots - WINDOW)
    count = (blocks[:, BLOCK - 1] - base) // WINDOW + 1
    col = jnp.broadcast_to(remote[:, None], (trips, 128))
    row = remote.reshape(steps, 1, BLOCK)

    def whole(shape):
        return pl.BlockSpec(shape, lambda i, *_: (0,) * len(shape), pipeline_mode=pl.Buffered(1))

    def blocked(cols):
        return pl.BlockSpec((BLOCK, cols), lambda i, *_: (i, 0))

    return pl.pallas_call(
        functools.partial(triplet_kernel, slots),
        grid_spec=pltpu.PrefetchScalarGridSpec(
            num_scalar_prefetch=2,
            grid=(steps,),
            in_specs=[
                blocked(128),
                pl.BlockSpec((1, 1, BLOCK), lambda i, *_: (i, 0, 0)),
                blocked(pair),
                whole((slots, pair)),
                whole((rows1, hid)),
                whole((hid, rows1)),
                whole((hid, width)),
                whole((width, hid)),
                whole((1, hid)),
            ],
            out_specs=[
                blocked(pair),
                whole((slots, pair)),
                whole((rows1 + width, hid)),
                whole((1, hid)),
            ],
            scratch_shapes=[
                pltpu.VMEM((slots, pair), F32),
                pltpu.VMEM((BLOCK, pair), F32),
            ],
        ),
        out_shape=[
            jax.ShapeDtypeStruct((trips, pair), BF16),
            jax.ShapeDtypeStruct((slots, pair), BF16),
            jax.ShapeDtypeStruct((rows1 + width, hid), F32),
            jax.ShapeDtypeStruct((1, hid), F32),
        ],
        compiler_params=pltpu.CompilerParams(
            dimension_semantics=("arbitrary",), vmem_limit_bytes=40 * 2**20
        ),
        cost_estimate=pl.CostEstimate(
            flops=2 * trips * 600000, bytes_accessed=20 * 2**20, transcendentals=trips * hid * 2
        ),
        name="triplets",
    )(base, count, col, row, own, far, w1, w1.T, w2, w2.T, bias[None, :])


def split(x):
    high = lax.reduce_precision(x, 8, 7)
    return high.astype(BF16), (x - high).astype(BF16)


def local(
    edges, cotangent, send_rows, send_count, trip_local, trip_remote, w_first, bias_first, w_second
):
    width = edges.shape[1]
    rows = edges.shape[0]
    ndev = lax.axis_size("phi") * lax.axis_size("eta")
    slots_per = send_rows.shape[2]
    slots = ndev * slots_per
    pair = 2 * width
    live = jnp.arange(slots_per, dtype=jnp.int32)[None, :] < send_count[0][:, None]
    chosen = jnp.where(live, send_rows[0], -1).reshape(slots)
    row_ids = jnp.arange(rows, dtype=jnp.int32)
    table = jnp.concatenate([edges, cotangent], axis=1)
    with jax.named_scope("pack"):
        hot = (chosen[:, None] == row_ids[None, :]).astype(BF16)
        outgoing = dot(hot, table).astype(BF16).reshape(ndev, slots_per, pair)
    arrived = lax.all_to_all(outgoing, AXES, split_axis=0, concat_axis=0, tiled=True)
    arrived = arrived.reshape(slots, pair)
    with jax.named_scope("order"):
        key = jnp.sort(trip_remote * rows + trip_local)
        remote = key // rows
        inner = key - remote * rows
    with jax.named_scope("own_rows"):
        own = dot((inner[:, None] == row_ids[None, :]).astype(BF16), table).astype(BF16)
    inner_sums, slot_sums, grads, gbias = triplets(
        remote, own, arrived, w_first, bias_first, w_second
    )
    hid = w_first.shape[1]
    per = grads.shape[0] // ndev
    high, low = split(grads)
    outbound = jnp.concatenate(
        [
            slot_sums.reshape(ndev, slots_per, pair),
            high.reshape(ndev, per, hid),
            low.reshape(ndev, per, hid),
        ],
        axis=1,
    )
    returned = lax.all_to_all(outbound, AXES, split_axis=0, concat_axis=0, tiled=True)
    with jax.named_scope("own_sums"):
        own_sum = dot((row_ids[:, None] == inner[None, :]).astype(BF16), inner_sums)
        own_sum = lax.optimization_barrier(table.astype(F32) + own_sum)
    mine = returned[:, slots_per:, :].astype(F32)
    mine = jnp.sum(mine[:, :per, :] + mine[:, per:, :], axis=0).astype(BF16)
    bias_high, bias_low = split(gbias)
    share = jnp.concatenate([mine, bias_high, bias_low, jnp.zeros((2, hid), BF16)], axis=0)
    share = jnp.broadcast_to(share[None], (ndev,) + share.shape)
    shared = lax.all_to_all(share, AXES, split_axis=0, concat_axis=0, tiled=True)
    with jax.named_scope("far_sums"):
        back = returned[:, :slots_per, :].reshape(slots, pair)
        far_sum = dot((row_ids[:, None] == chosen[None, :]).astype(BF16), back)
    both = (own_sum + far_sum).astype(BF16)
    total = shared[:, :per, :].reshape(ndev * per, hid).astype(F32)
    cut = w_first.shape[0]
    grad_bias = jnp.sum(shared[:, per : per + 2, :].astype(F32), axis=(0, 1))
    return (both[:, :width], both[:, width:], total[:cut], grad_bias, total[cut:].T)


def solution(mesh):
    in_specs = (
        P(AXES, None),
        P(AXES, None),
        P(AXES, None, None),
        P(AXES, None),
        P(AXES),
        P(AXES),
        P(),
        P(),
        P(),
    )
    out_specs = (P(AXES, None), P(AXES, None), P(), P(), P())
    return jax.shard_map(local, mesh=mesh, in_specs=in_specs, out_specs=out_specs, check_vma=False)
```

time: 577 us -> 162 us (0.28)
  other arithmetic: 254 us -> 13.6 us
  local copies, waits for them, and re-layouts: 158 us -> 14.8 us
  blocking collectives: 67.5 us -> 0 us
  Pallas kernels: 0 us -> 35.2 us
  between operations: 14.3 us -> 0.88 us
  matrix products: 32 us -> 43.4 us
    scatter-add x6 -> x0, other arithmetic: 226 us -> none  [the longest x1 46.4 us: local(): slot_grad = jax.ops.segment_sum(d_outer, trip_remote, ndev * slots_per)]
    gather x4 -> x0, local copies, waits for them, and re-layouts: 139 us -> none  [the longest x1 53.3 us: local(): outer_pair = arrived[trip_remote]]
    psum x1 -> x0, blocking collectives: 67.5 us -> none  [local(): lax.psum((grad_first, grad_bias, grad_second), ('phi', 'eta'))]
    pallas_call x0 -> x1, Pallas kernels: none -> 35.2 us  [triplets(): pl.pallas_call(functools.partial(triplet_kernel, slots), grid_spec=pltpu....]
    all_to_all x2 -> x3, waiting for transfers between devices: 0.01 us -> 31.2 us  [the longest x1 19.3 us: local(): lax.all_to_all(outbound, AXES, split_axis=0, concat_axis=0, tiled=True)]
    psum x1 -> x0, waiting for transfers between devices: 28.6 us -> none  [local(): lax.psum((grad_first, grad_bias, grad_second), ('phi', 'eta'))]
    convert_element_type x6 -> x4, other arithmetic: 13.3 us -> 1.26 us  [the longest x1 1.11 us: local(): mine = returned[:, slots_per:, :].astype(F32)]
    dot_general x6 -> x4, matrix products: 32 us -> 43.4 us  [dot(): return jnp.dot(a, b, preferred_element_type=F32)]
  transfers between devices with their start and end apart: 3 -> 3, of which waited for: 1 -> 3; matrix products, arithmetic and copies ran while one was open for 36% -> 29% of each run, Pallas kernels for 0% -> 0%
where the time goes in v1:
time: 162 us; the launch traced here: 161 us
  matrix products  43.4 us (27%)
  Pallas kernels  35.2 us (22%)
  waiting for transfers between devices  31.2 us (19%)
  starting transfers between devices  21.8 us (13%)
  local copies, waits for them, and re-layouts  14.8 us (9%)
  other arithmetic  13.6 us (8%)
    dot_general x4, matrix products, dot(): return jnp.dot(a, b, preferred_element_type=F32)  43.4 us
    pallas_call x1, Pallas kernels, triplets(): pl.pallas_call(functools.partial(triplet_kernel, slots), grid_spec=pltpu....  35.2 us
    all_to_all x1, waiting for transfers between devices, local(): lax.all_to_all(outbound, AXES, split_axis=0, concat_axis=0, tiled=True)  19.3 us
    all_to_all x1, starting transfers between devices, local(): lax.all_to_all(outgoing, AXES, split_axis=0, concat_axis=0, tiled=True)  11.5 us
    all_to_all x1, waiting for transfers between devices, local(): lax.all_to_all(outgoing, AXES, split_axis=0, concat_axis=0, tiled=True)  8.23 us
    unnamed x23, local copies, waits for them, and re-layouts  7.18 us
    sort x1, other arithmetic, local(): key = jnp.sort(trip_remote * rows + trip_local)  6.77 us
    all_to_all x1, starting transfers between devices, local(): lax.all_to_all(outbound, AXES, split_axis=0, concat_axis=0, tiled=True)  5.59 us
  transfers between devices with their start and end apart: 3, of which 3 were waited for; matrix products, arithmetic and copies ran while one was open for 29% of the time, Pallas kernels for 0%

profile of v1, /device:TPU:1, one launch (start us, length us, event | category | flops | bytes accessed | tf_op | source)
XLA Modules:
  0.0 161.0 jit_solution(5905013538671139968)
XLA Ops:
  0.6 1.1 constant_dynamic-update-slice_fusion.1
  3.5 1.2 constant_dynamic-update-slice_fusion
  4.7 0.9 copy-done.5
  5.6 6.8 %fusion.9 = bf16[4096,256]{1,0:T(8,128)(2,1)} fusion(bf16[2048,256]{1,0:T(8,128)(2,1)S(1)} %constant_dynamic-update-slice_fusion, s32[4096]{0:T(1024)S(1)} %broadcast_select_fusion), kind=kOutput, calls=%fused_computation.13 | convolution fusion | flops 4304404480 | bytes 3162112 | tf_op jit(solution)/shard_map/pack/dot_general | solution.py:18
  12.5 11.5 %all-to-all-start = ((bf16[128,32,256]{2,1,0:T(8,128)(2,1)}), bf16[128,32,256]{2,1,0:T(8,128)(2,1)S(1)}, u32[]{:S(2)}, u32[]{:S(2)}) async-start(bf16[128,32,256]{2,1,0:T(8,128)(2,1)} %bitcast.20), calls=%async_computation | async-start | bytes 4194304 | tf_op jit(solution)/shard_map/all_to_all | solution.py:215
  24.0 6.8 %sort.15 = (s32[8192]{0:T(1024)S(1)}, s32[8192]{0:T(1024)}) sort(s32[8192]{0:T(1024)S(1)} %multiply_add_fusion, s32[8192]{0:T(1024)S(1)} %iota.17), dimensions={0}, to_apply=%region_0.1 | sort | flops 106496 | bytes 131072 | tf_op jit(solution)/shard_map/order/jit(sort)/sort | solution.py:218
  31.4 14.0 %fusion.8.own_ref = bf16[8192,256]{1,0:T(8,128)(2,1)} fusion(bf16[2048,256]{1,0:T(8,128)(2,1)} %copy-done.5, s32[8192]{0:T(1024)S(1)} %get-tuple-element.34), kind=kOutput, calls=%fused_computation.12 | convolution fusion | flops 8608808960 | bytes 5275648 | tf_op jit(solution)/shard_map/own_rows/dot_general | solution.py:18
  45.4 8.2 %all-to-all-done = bf16[128,32,256]{2,1,0:T(8,128)(2,1)S(1)} async-done(((bf16[128,32,256]{2,1,0:T(8,128)(2,1)}), bf16[128,32,256]{2,1,0:T(8,128)(2,1)S(1)}, u32[]{:S(2)}, u32[]{:S(2)}) %all-to-all-start) | async-done | bytes 2097184 | tf_op jit(solution)/shard_map/all_to_all | solution.py:215
  53.6 1.2 broadcast_in_dim.12.col_ref
  54.9 35.2 %triplets.1 = (bf16[8192,256]{1,0:T(8,128)(2,1)S(1)}, bf16[4096,256]{1,0:T(8,128)(2,1)S(1)}, f32[512,256]{1,0:T(8,128)S(1)}, f32[1,256]{1,0:T(1,128)S(1)}) custom-call(s32[32]{0:T(128)S(1)} %get-tuple-element.29.base_ref, s32[32]{0:T(128)S(1)} %get-tuple-element.28.count_ref, s32[8192,128]{1,0:T(8,128)S(1)} %broadcast_in_dim.12.col_ref, ...), custom_call_target="tpu_custom_call" | custom-call | flops 9830400000 | bytes 20971520 | tf_op jit(solution)/shard_map/triplets/pallas_call | solution.py:151
  90.1 1.3 copy-done
  91.5 1.9 %copy-done.4 = bf16[8192,256]{1,0:T(8,128)(2,1)} copy-done((bf16[8192,256]{1,0:T(8,128)(2,1)}, bf16[8192,256]{1,0:T(8,128)(2,1)S(1)}, u32[]{:S(2)}) %copy-start.4) | copy-done | bytes 4194328
  93.6 3.7 %pad_maximum_fusion = bf16[128,40,256]{2,1,0:T(8,128)(2,1)} fusion(bf16[128,4,256]{2,1,0:T(4,128)(2,1)S(1)} %reshape.86, bf16[128,4,256]{2,1,0:T(4,128)(2,1)S(1)} %reshape.85, bf16[128,32,256]{2,1,0:T(8,128)(2,1)} %bitcast.15), kind=kLoop, calls=%fused_computation.16 | loop fusion | flops 7864320 | bytes 5242880 | tf_op jit(solution)/shard_map/concatenate | solution.py:229
  97.3 5.6 %all-to-all-start.1 = ((bf16[128,40,256]{2,1,0:T(8,128)(2,1)}), bf16[128,40,256]{2,1,0:T(8,128)(2,1)}, u32[]{:S(2)}, u32[]{:S(2)}) async-start(bf16[128,40,256]{2,1,0:T(8,128)(2,1)} %pad_maximum_fusion), calls=%async_computation.1 | async-start | bytes 5242880 | tf_op jit(solution)/shard_map/all_to_all | solution.py:237
  103.0 15.7 %fusion.10 = f32[2048,256]{1,0:T(8,128)} fusion(bf16[8192,256]{1,0:T(8,128)(2,1)} %copy-done.4, s32[8192]{0:T(1024)S(1)} %get-tuple-element.34, bf16[2048,256]{1,0:T(8,128)(2,1)S(1)} %copy-done.6), kind=kOutput, calls=%fused_computation.14 | convolution fusion | flops 8607760384 | bytes 7372800 | tf_op jit(solution)/shard_map/own_sums/dot_general | solution.py:18
  118.7 19.3 %all-to-all-done.1 = bf16[128,40,256]{2,1,0:T(8,128)(2,1)} async-done(((bf16[128,40,256]{2,1,0:T(8,128)(2,1)}), bf16[128,40,256]{2,1,0:T(8,128)(2,1)}, u32[]{:S(2)}, u32[]{:S(2)}) %all-to-all-start.1) | async-done | bytes 2621472 | tf_op jit(solution)/shard_map/all_to_all | solution.py:237
  138.0 1.1 slice_convert_fusion
  139.4 0.8 broadcast_in_dim.16
  140.2 4.8 %all-to-all-start.2 = ((bf16[128,8,256]{2,1,0:T(8,128)(2,1)}), bf16[128,8,256]{2,1,0:T(8,128)(2,1)S(1)}, u32[]{:S(2)}, u32[]{:S(2)}) async-start(bf16[128,8,256]{2,1,0:T(8,128)(2,1)} %broadcast_in_dim.16), calls=%async_computation.2 | async-start | bytes 1048576 | tf_op jit(solution)/shard_map/all_to_all | solution.py:246
  145.0 1.8 %slice.58 = bf16[128,32,256]{2,1,0:T(8,128)(2,1)S(1)} slice(bf16[128,40,256]{2,1,0:T(8,128)(2,1)} %all-to-all-done.1), slice={[0:128], [0:32], [0:256]} | slice | bytes 4194304 | tf_op jit(solution)/shard_map/far_sums/slice | solution.py:248
  146.8 6.9 %fusion.12 = bf16[2048,256]{1,0:T(8,128)(2,1)S(1)} fusion(f32[2048,256]{1,0:T(8,128)} %fusion.10, bf16[4096,256]{1,0:T(8,128)(2,1)S(1)} %bitcast.21, s32[4096]{0:T(1024)S(1)} %broadcast_select_fusion), kind=kOutput, calls=%fused_computation.17 | convolution fusion | flops 4304404480 | bytes 5259264 | tf_op jit(solution)/shard_map/far_sums/dot_general | solution.py:18
  153.7 1.0 fusion.19
  154.7 3.7 %all-to-all-done.2 = bf16[128,8,256]{2,1,0:T(8,128)(2,1)S(1)} async-done(((bf16[128,8,256]{2,1,0:T(8,128)(2,1)}), bf16[128,8,256]{2,1,0:T(8,128)(2,1)S(1)}, u32[]{:S(2)}, u32[]{:S(2)}) %all-to-all-start.2) | async-done | bytes 524320 | tf_op jit(solution)/shard_map/all_to_all | solution.py:246
  158.5 0.9 slice.52
  (42 shorter events, 4.6 us)
Async XLA Ops:
  4.7 1.0 copy-start.5
  12.5 11.5 %copy-start.7 = (s32[8192]{0:T(1024)S(1)}, s32[8192]{0:T(1024)}, u32[]{:S(2)}) copy-start(s32[8192]{0:T(1024)} %param.13) | copy-start | bytes 98308
  12.5 11.5 %copy-start.8 = (s32[8192]{0:T(1024)S(1)}, s32[8192]{0:T(1024)}, u32[]{:S(2)}) copy-start(s32[8192]{0:T(1024)} %param.14) | copy-start | bytes 98308
  12.5 18.6 %copy-start.1 = (bf16[384,256]{1,0:T(8,128)(2,1)S(1)}, bf16[384,256]{1,0:T(8,128)(2,1)}, u32[]{:S(2)}) copy-start(bf16[384,256]{1,0:T(8,128)(2,1)} %w1_ref.1) | copy-start | bytes 589828
  12.5 18.7 %copy-start.2 = (bf16[256,128]{1,0:T(8,128)(2,1)S(1)}, bf16[256,128]{1,0:T(8,128)(2,1)}, u32[]{:S(2)}) copy-start(bf16[256,128]{1,0:T(8,128)(2,1)} %w2_ref.1) | copy-start | bytes 196612
  12.5 41.2 %all-to-all-start = ((bf16[128,32,256]{2,1,0:T(8,128)(2,1)}), bf16[128,32,256]{2,1,0:T(8,128)(2,1)S(1)}, u32[]{:S(2)}, u32[]{:S(2)}) async-start(bf16[128,32,256]{2,1,0:T(8,128)(2,1)} %bitcast.20), calls=%async_computation | async-start | bytes 4194304 | tf_op jit(solution)/shard_map/all_to_all | solution.py:215
  45.4 9.5 %copy-start.3 = (f32[256]{0:T(256)S(1)}, f32[256]{0:T(256)}, u32[]{:S(2)}) copy-start(f32[256]{0:T(256)} %param.16) | copy-start | bytes 3076
  90.1 1.3 copy-start
  91.5 1.9 %copy-start.4 = (bf16[8192,256]{1,0:T(8,128)(2,1)}, bf16[8192,256]{1,0:T(8,128)(2,1)S(1)}, u32[]{:S(2)}) copy-start(bf16[8192,256]{1,0:T(8,128)(2,1)S(1)} %get-tuple-element.12) | copy-start | bytes 12582916
  93.6 9.4 %copy-start.6 = (bf16[2048,256]{1,0:T(8,128)(2,1)S(1)}, bf16[2048,256]{1,0:T(8,128)(2,1)}, u32[]{:S(2)}) copy-start(bf16[2048,256]{1,0:T(8,128)(2,1)} %copy-done.5) | copy-start | bytes 3145732
  97.3 40.6 %all-to-all-start.1 = ((bf16[128,40,256]{2,1,0:T(8,128)(2,1)}), bf16[128,40,256]{2,1,0:T(8,128)(2,1)}, u32[]{:S(2)}, u32[]{:S(2)}) async-start(bf16[128,40,256]{2,1,0:T(8,128)(2,1)} %pad_maximum_fusion), calls=%async_computation.1 | async-start | bytes 5242880 | tf_op jit(solution)/shard_map/all_to_all | solution.py:237
  140.2 18.2 %all-to-all-start.2 = ((bf16[128,8,256]{2,1,0:T(8,128)(2,1)}), bf16[128,8,256]{2,1,0:T(8,128)(2,1)S(1)}, u32[]{:S(2)}, u32[]{:S(2)}) async-start(bf16[128,8,256]{2,1,0:T(8,128)(2,1)} %broadcast_in_dim.16), calls=%async_computation.2 | async-start | bytes 1048576 | tf_op jit(solution)/shard_map/all_to_all | solution.py:246

commit v2 on v1

v2 whole, which is shorter than its diff:
```python
import functools

import jax
import jax.numpy as jnp
from jax import lax
from jax.experimental import pallas as pl
from jax.experimental.pallas import tpu as pltpu
from jax.sharding import PartitionSpec as P

AXES = ("phi", "eta")
BLOCK = 2048
SUPER = 2048
CHUNK = 512
ORDER = (3, 2, 1, 0)
PART = 256
WINDOW = 256
BF16 = jnp.bfloat16
F32 = jnp.float32


def dot(a, b):
    return jnp.dot(a, b, preferred_element_type=F32)


def dot_rows(a, b):
    return lax.dot_general(a, b, (((0,), (0,)), ((), ())), preferred_element_type=F32)


def triplet_kernel(
    base_ref,
    count_ref,
    most_ref,
    row_ref,
    own_hbm,
    far_ref,
    w1_ref,
    w1t_ref,
    w2_ref,
    w2t_ref,
    bias_ref,
    inner_ref,
    out_ref,
    gbias_ref,
    total_ref,
    grad_ref,
    far2_ref,
    outer_ref,
    own_ref,
    own_sem,
):
    fetch = pltpu.make_async_copy(own_hbm, own_ref, own_sem)
    fetch.start()
    width = own_ref.shape[1] // 2
    slots = far_ref.shape[0]
    parts = BLOCK // PART
    ndev, _, pair = out_ref.shape
    slots_per = slots // ndev

    total_ref[...] = jnp.zeros_like(total_ref)
    grad_ref[...] = jnp.zeros_like(grad_ref)
    gbias_ref[...] = jnp.zeros_like(gbias_ref)

    def window(part, w):
        first = base_ref[part] + w * WINDOW
        start = pl.multiple_of(jnp.minimum(first, slots - WINDOW), 16)
        rel = row_ref[part] - start
        if not isinstance(w, int):
            rel = jnp.where(rel >= first - start, rel, -1)
        down = lax.broadcasted_iota(jnp.int32, (WINDOW, PART), 0)
        return pl.ds(start, WINDOW), (down == rel).astype(F32).astype(BF16)

    def place(part):
        return pl.ds(pl.multiple_of(part * PART, PART), PART)

    def gather(step, carry):
        for j in range(parts):
            part = step * parts + j
            span, hot = window(part, 0)
            far2_ref[place(part), :] = dot_rows(hot, far_ref[span, :]).astype(BF16)

        @pl.when(most_ref[step] > 1)
        def _():
            for j in range(parts):
                part = step * parts + j

                def more(w, carry):
                    span, hot = window(part, w)
                    far2_ref[place(part), :] += dot_rows(hot, far_ref[span, :]).astype(BF16)
                    return carry

                lax.fori_loop(1, count_ref[part], more, 0)

        return carry

    def mlp(step, carry):
        chunks = SUPER // CHUNK
        state = [dict() for _ in range(chunks)]

        def here(c):
            return pl.ds(pl.multiple_of(step * SUPER + c * CHUNK, CHUNK), CHUNK)

        def stage0(c):
            v = state[c]
            a = own_ref[here(c), :width]
            b = far2_ref[here(c), :width]
            prod = (a.astype(F32) * b.astype(F32)).astype(BF16)
            v["x"] = jnp.concatenate([a, b, prod], axis=1)
            v["pre"] = dot(v["x"], w1_ref[...]) + bias_ref[...]
            ga = own_ref[here(c), width:]
            gb = far2_ref[here(c), width:]
            v["dm"] = (ga.astype(F32) + gb.astype(F32)).astype(BF16)
            v["dh"] = dot(v["dm"], w2t_ref[...])

        def stage1(c):
            v = state[c]
            pre = v.pop("pre")
            sig = 0.5 * jnp.tanh(0.5 * pre) + 0.5
            v["h"] = (pre * sig).astype(BF16)
            dpre = v.pop("dh") * (sig * (1.0 + pre * (1.0 - sig)))
            gbias_ref[...] += jnp.sum(dpre, axis=0, keepdims=True)
            v["dpre"] = dpre.astype(BF16)

        def stage2(c):
            v = state[c]
            mb = dot(v["h"], w2_ref[...]).astype(BF16)
            inner_ref[here(c), :width] = mb
            outer_ref[here(c), :width] = mb
            v["dx"] = dot(v["dpre"], w1t_ref[...])

        def stage3(c):
            v = state[c]
            dx = v.pop("dx")
            af = own_ref[here(c), :width].astype(F32)
            b = far2_ref[here(c), :width].astype(F32)
            dprod = dx[:, 2 * width :]
            inner_ref[here(c), width:] = (dx[:, :width] + dprod * b).astype(BF16)
            outer_ref[here(c), width:] = (dx[:, width : 2 * width] + dprod * af).astype(BF16)
            rows1 = w1_ref.shape[0]
            grad_ref[:rows1, :] += dot_rows(v["x"], v["dpre"])
            grad_ref[rows1:, :] += dot_rows(v["dm"], v["h"])

        stages = [stage0, stage1, stage2, stage3]
        for t in range(chunks + len(stages) - 1):
            for s in ORDER:
                c = t - s
                if 0 <= c < chunks:
                    stages[s](c)
        return carry

    def scatter(step, carry):
        for j in range(parts):
            part = step * parts + j
            span, hot = window(part, 0)
            total_ref[span, :] += dot(hot, outer_ref[place(part), :])

        @pl.when(most_ref[step] > 1)
        def _():
            for j in range(parts):
                part = step * parts + j

                def more(w, carry):
                    span, hot = window(part, w)
                    total_ref[span, :] += dot(hot, outer_ref[place(part), :])
                    return carry

                lax.fori_loop(1, count_ref[part], more, 0)

        return carry

    trips = own_ref.shape[0]
    lax.fori_loop(0, trips // BLOCK, gather, 0)
    fetch.wait()
    lax.fori_loop(0, trips // SUPER, mlp, 0)
    lax.fori_loop(0, trips // BLOCK, scatter, 0)

    def close(d, carry):
        out_ref[d, :slots_per, :] = total_ref[
            pl.ds(pl.multiple_of(d * slots_per, slots_per), slots_per), :
        ].astype(BF16)
        return carry

    lax.fori_loop(0, ndev, close, 0, unroll=8)

    def close_grad(k, carry):
        for c in range(2):
            g = grad_ref[pl.ds(pl.multiple_of(k * 8, 8), 8), c * 128 : (c + 1) * 128]
            high = g.astype(BF16)
            low = (g - high.astype(F32)).astype(BF16)
            out_ref[2 * k + c, slots_per:, :] = jnp.concatenate([high, low], axis=1)
        return carry

    lax.fori_loop(0, ndev // 2, close_grad, 0, unroll=4)


def triplets(remote, own, far, w1, bias, w2, ndev):
    trips = remote.shape[0]
    slots, pair = far.shape
    width = pair // 2
    hid = w1.shape[1]
    rows1 = w1.shape[0]
    steps = trips // BLOCK
    parts = BLOCK // PART
    blocks = remote.reshape(steps * parts, PART)
    base = jnp.minimum(blocks[:, 0] // 16 * 16, slots - WINDOW)
    count = (blocks[:, PART - 1] - base) // WINDOW + 1
    most = jnp.max(count.reshape(steps, parts), axis=1)
    row = remote.reshape(steps * parts, 1, PART)
    smem = pl.BlockSpec(memory_space=pltpu.SMEM)
    vmem = pl.BlockSpec(memory_space=pltpu.VMEM)
    return pl.pallas_call(
        triplet_kernel,
        in_specs=[smem] * 3 + [vmem, pl.BlockSpec(memory_space=pl.ANY)] + [vmem] * 6,
        out_specs=[vmem] * 3,
        scratch_shapes=[
            pltpu.VMEM((slots, pair), F32),
            pltpu.VMEM((rows1 + width, hid), F32),
            pltpu.VMEM((trips, pair), BF16),
            pltpu.VMEM((trips, pair), BF16),
            pltpu.VMEM((trips, pair), BF16),
            pltpu.SemaphoreType.DMA,
        ],
        out_shape=[
            jax.ShapeDtypeStruct((trips, pair), BF16),
            jax.ShapeDtypeStruct((ndev, slots // ndev + 8, pair), BF16),
            jax.ShapeDtypeStruct((1, hid), F32),
        ],
        compiler_params=pltpu.CompilerParams(vmem_limit_bytes=36 * 2**20),
        cost_estimate=pl.CostEstimate(
            flops=2 * trips * 600000, bytes_accessed=20 * 2**20, transcendentals=trips * hid
        ),
        name="triplets",
    )(base, count, most, row, own, far, w1, w1.T, w2, w2.T, bias[None, :])


def split(x):
    high = lax.reduce_precision(x, 8, 7)
    return high.astype(BF16), (x - high).astype(BF16)


def local(
    edges, cotangent, send_rows, send_count, trip_local, trip_remote, w_first, bias_first, w_second
):
    width = edges.shape[1]
    rows = edges.shape[0]
    ndev = lax.axis_size("phi") * lax.axis_size("eta")
    slots_per = send_rows.shape[2]
    slots = ndev * slots_per
    pair = 2 * width
    live = jnp.arange(slots_per, dtype=jnp.int32)[None, :] < send_count[0][:, None]
    chosen = jnp.where(live, send_rows[0], -1).reshape(slots)
    row_ids = jnp.arange(rows, dtype=jnp.int32)
    table = jnp.concatenate([edges, cotangent], axis=1)
    with jax.named_scope("pack"):
        hot = (chosen[:, None] == row_ids[None, :]).astype(BF16)
        outgoing = dot(hot, table).astype(BF16).reshape(ndev, slots_per, pair)
    arrived = lax.all_to_all(outgoing, AXES, split_axis=0, concat_axis=0, tiled=True)
    arrived = arrived.reshape(slots, pair)
    with jax.named_scope("order"):
        key = jnp.sort(trip_remote * rows + trip_local)
        remote = key // rows
        inner = key - remote * rows
    with jax.named_scope("own_rows"):
        own = dot((inner[:, None] == row_ids[None, :]).astype(BF16), table).astype(BF16)
    inner_sums, outbound, gbias = triplets(
        remote, own, arrived, w_first, bias_first, w_second, ndev
    )
    returned = lax.all_to_all(outbound, AXES, split_axis=0, concat_axis=0, tiled=True)
    with jax.named_scope("own_sums"):
        own_sum = dot((row_ids[:, None] == inner[None, :]).astype(BF16), inner_sums)
        own_sum = lax.optimization_barrier(table.astype(F32) + own_sum)
    hid = w_first.shape[1]
    mine = jnp.sum(returned[:, slots_per:, :].astype(F32), axis=0)
    mine = (mine[:, :width] + mine[:, width:]).astype(BF16)
    bias_high, bias_low = split(gbias)
    ends = jnp.concatenate([bias_high, bias_low], axis=0).reshape(4, width)
    ends = jnp.pad(ends, ((0, 4), (0, 0)))
    share = jnp.concatenate([mine, ends], axis=1)
    share = jnp.broadcast_to(share[None], (ndev,) + share.shape)
    shared = lax.all_to_all(share, AXES, split_axis=0, concat_axis=0, tiled=True)
    with jax.named_scope("far_sums"):
        back = returned[:, :slots_per, :].reshape(slots, pair)
        far_sum = dot((row_ids[:, None] == chosen[None, :]).astype(BF16), back)
    both = (own_sum + far_sum).astype(BF16)
    total = shared[:, :, :width].astype(F32).reshape(ndev // 2, 2, 8, width)
    total = total.transpose(0, 2, 1, 3).reshape(ndev * 4, hid)
    cut = w_first.shape[0]
    grad_bias = jnp.sum(shared[:, :4, width:].astype(F32), axis=0).reshape(2, hid).sum(0)
    return (both[:, :width], both[:, width:], total[:cut], grad_bias, total[cut:].T)


def solution(mesh):
    in_specs = (
        P(AXES, None),
        P(AXES, None),
        P(AXES, None, None),
        P(AXES, None),
        P(AXES),
        P(AXES),
        P(),
        P(),
        P(),
    )
    out_specs = (P(AXES, None), P(AXES, None), P(), P(), P())
    return jax.shard_map(local, mesh=mesh, in_specs=in_specs, out_specs=out_specs, check_vma=False)
```

time: 162 us -> 137 us (0.85)
  Pallas kernels: 35.2 us -> 17.7 us
  other arithmetic: 13.6 us -> 8.64 us
  waiting for transfers between devices: 31.2 us -> 34.4 us
  matrix products: 43.4 us -> 40.4 us
  local copies, waits for them, and re-layouts: 14.8 us -> 13.1 us
    pallas_call x1, Pallas kernels: 35.2 us -> 17.7 us  [triplets(): pl.pallas_call(triplet_kernel, in_specs=[smem] * 3 + [vmem, pl.BlockSpec(...]
    concatenate x2, other arithmetic: 3.79 us -> 0.02 us  [the longest x1 0.01 us: local(): ends = jnp.concatenate([bias_high, bias_low], axis=0).reshape(4, width)]
    dot_general x4, matrix products: 43.4 us -> 40.4 us  [dot(): return jnp.dot(a, b, preferred_element_type=F32)]
    all_to_all x1, waiting for transfers between devices: 19.3 us -> 21.3 us  [local(): lax.all_to_all(outbound, AXES, split_axis=0, concat_axis=0, tiled=True)]
  transfers between devices with their start and end apart: 3 -> 3, of which waited for: 3 -> 3; matrix products, arithmetic and copies ran while one was open for 29% -> 31% of each run, Pallas kernels for 0% -> 0%
where the time goes in v2:
time: 137 us; the launch traced here: 136 us
  matrix products  40.4 us (29%)
  waiting for transfers between devices  34.4 us (25%)
  starting transfers between devices  20.9 us (15%)
  Pallas kernels  17.7 us (13%)
  local copies, waits for them, and re-layouts  13.1 us (10%)
  other arithmetic  8.64 us (6%)
    dot_general x4, matrix products, dot(): return jnp.dot(a, b, preferred_element_type=F32)  40.4 us
    all_to_all x1, waiting for transfers between devices, local(): lax.all_to_all(outbound, AXES, split_axis=0, concat_axis=0, tiled=True)  21.3 us
    pallas_call x1, Pallas kernels, triplets(): pl.pallas_call(triplet_kernel, in_specs=[smem] * 3 + [vmem, pl.BlockSpec(...  17.7 us
    all_to_all x1, starting transfers between devices, local(): lax.all_to_all(outgoing, AXES, split_axis=0, concat_axis=0, tiled=True)  11.5 us
    unnamed x23, local copies, waits for them, and re-layouts  8.41 us
    all_to_all x1, waiting for transfers between devices, local(): lax.all_to_all(outgoing, AXES, split_axis=0, concat_axis=0, tiled=True)  7.9 us
    sort x1, other arithmetic, local(): key = jnp.sort(trip_remote * rows + trip_local)  6.77 us
    all_to_all x1, waiting for transfers between devices, local(): lax.all_to_all(share, AXES, split_axis=0, concat_axis=0, tiled=True)  5.11 us
  transfers between devices with their start and end apart: 3, of which 3 were waited for; matrix products, arithmetic and copies ran while one was open for 31% of the time, Pallas kernels for 0%

profile of v2, /device:TPU:1, one launch (start us, length us, event | category | flops | bytes accessed | tf_op | source)
XLA Modules:
  0.0 136.0 jit_solution(1145768631004689653)
XLA Ops:
  0.6 0.7 iota_compare_fusion.18
  1.5 0.8 copy.25
  2.4 1.1 constant_dynamic-update-slice_fusion.1
  3.5 1.2 constant_dynamic-update-slice_fusion
  4.7 6.9 %fusion.9 = bf16[4096,256]{1,0:T(8,128)(2,1)} fusion(bf16[2048,256]{1,0:T(8,128)(2,1)S(1)} %constant_dynamic-update-slice_fusion, s32[4096]{0:T(1024)S(1)} %broadcast_select_fusion), kind=kOutput, calls=%fused_computation.13 | convolution fusion | flops 4304404480 | bytes 3162112 | tf_op jit(solution)/shard_map/pack/dot_general | solution.py:22
  11.6 11.5 %all-to-all-start = ((bf16[128,32,256]{2,1,0:T(8,128)(2,1)}), bf16[128,32,256]{2,1,0:T(8,128)(2,1)S(1)}, u32[]{:S(2)}, u32[]{:S(2)}) async-start(bf16[128,32,256]{2,1,0:T(8,128)(2,1)} %bitcast.27), calls=%async_computation | async-start | bytes 4194304 | tf_op jit(solution)/shard_map/all_to_all | solution.py:256
  23.2 6.8 %sort.15 = (s32[8192]{0:T(1024)S(1)}, s32[8192]{0:T(1024)}) sort(s32[8192]{0:T(1024)S(1)} %multiply_add_fusion, s32[8192]{0:T(1024)S(1)} %iota.17), dimensions={0}, to_apply=%region_0.1 | sort | flops 106496 | bytes 131072 | tf_op jit(solution)/shard_map/order/jit(sort)/sort | solution.py:259
  30.8 14.0 %fusion.8.own_hbm = bf16[8192,256]{1,0:T(8,128)(2,1)} fusion(bf16[2048,256]{1,0:T(8,128)(2,1)} %copy-done.5, s32[8192]{0:T(1024)S(1)} %get-tuple-element.35), kind=kOutput, calls=%fused_computation.12 | convolution fusion | flops 8608808960 | bytes 5275648 | tf_op jit(solution)/shard_map/own_rows/dot_general | solution.py:22
  44.9 7.9 %all-to-all-done = bf16[128,32,256]{2,1,0:T(8,128)(2,1)S(1)} async-done(((bf16[128,32,256]{2,1,0:T(8,128)(2,1)}), bf16[128,32,256]{2,1,0:T(8,128)(2,1)S(1)}, u32[]{:S(2)}, u32[]{:S(2)}) %all-to-all-start) | async-done | bytes 2097184 | tf_op jit(solution)/shard_map/all_to_all | solution.py:256
  52.8 2.2 %copy-done.4 = bf16[8192,256]{1,0:T(8,128)(2,1)S(1)} copy-done((bf16[8192,256]{1,0:T(8,128)(2,1)S(1)}, bf16[8192,256]{1,0:T(8,128)(2,1)}, u32[]{:S(2)}) %copy-start.4) | copy-done | bytes 4194328
  55.0 17.7 %triplets.1 = (bf16[8192,256]{1,0:T(8,128)(2,1)S(1)}, bf16[128,40,256]{2,1,0:T(8,128)(2,1)}, f32[1,256]{1,0:T(1,128)S(1)}) custom-call(s32[32]{0:T(128)S(1)} %get-tuple-element.32.base_ref, s32[32]{0:T(128)S(1)} %get-tuple-element.31.count_ref, s32[4]{0:T(128)S(1)} %fusion.24.most_ref, s32[32,1,256]{2,1,0:T(1,128)S(1)} %bitcast.24, ...), custom_call_target="tpu_custom_call" | custom-call | flops 9830400000 | bytes 20971520 | tf_op jit(solution)/shard_map/triplets/pallas_call | solution.py:210
  72.7 1.9 %copy-done.3 = bf16[8192,256]{1,0:T(8,128)(2,1)} copy-done((bf16[8192,256]{1,0:T(8,128)(2,1)}, bf16[8192,256]{1,0:T(8,128)(2,1)S(1)}, u32[]{:S(2)}) %copy-start.3) | copy-done | bytes 4194328
  74.6 4.7 %all-to-all-start.1 = ((bf16[128,40,256]{2,1,0:T(8,128)(2,1)}), bf16[128,40,256]{2,1,0:T(8,128)(2,1)S(1)}, u32[]{:S(2)}, u32[]{:S(2)}) async-start(bf16[128,40,256]{2,1,0:T(8,128)(2,1)} %get-tuple-element.12), calls=%async_computation.1 | async-start | bytes 5242880 | tf_op jit(solution)/shard_map/all_to_all | solution.py:267
  79.3 13.8 %fusion.10 = f32[2048,256]{1,0:T(8,128)} fusion(bf16[8192,256]{1,0:T(8,128)(2,1)} %copy-done.3, s32[8192]{0:T(1024)S(1)} %get-tuple-element.35, bf16[2048,256]{1,0:T(8,128)(2,1)} %copy-done.5), kind=kOutput, calls=%fused_computation.14 | convolution fusion | flops 8607760384 | bytes 7372800 | tf_op jit(solution)/shard_map/own_sums/dot_general | solution.py:22
  93.1 21.3 %all-to-all-done.1 = bf16[128,40,256]{2,1,0:T(8,128)(2,1)S(1)} async-done(((bf16[128,40,256]{2,1,0:T(8,128)(2,1)}), bf16[128,40,256]{2,1,0:T(8,128)(2,1)S(1)}, u32[]{:S(2)}, u32[]{:S(2)}) %all-to-all-start.1) | async-done | bytes 2621472 | tf_op jit(solution)/shard_map/all_to_all | solution.py:267
  114.7 0.8 broadcast_in_dim.10
  115.5 4.8 %all-to-all-start.2 = ((bf16[128,8,256]{2,1,0:T(8,128)(2,1)}), bf16[128,8,256]{2,1,0:T(8,128)(2,1)S(1)}, u32[]{:S(2)}, u32[]{:S(2)}) async-start(bf16[128,8,256]{2,1,0:T(8,128)(2,1)} %broadcast_in_dim.10), calls=%async_computation.2 | async-start | bytes 1048576 | tf_op jit(solution)/shard_map/all_to_all | solution.py:279
  120.5 1.3 copy-done.8
  121.8 5.7 %fusion.12 = bf16[2048,256]{1,0:T(8,128)(2,1)S(1)} fusion(f32[2048,256]{1,0:T(8,128)S(1)} %copy-done.8, bf16[4096,256]{1,0:T(8,128)(2,1)S(1)} %bitcast.28, s32[4096]{0:T(1024)S(1)} %broadcast_select_fusion), kind=kOutput, calls=%fused_computation.16 | convolution fusion | flops 4304404480 | bytes 5259264 | tf_op jit(solution)/shard_map/far_sums/dot_general | solution.py:22
  127.5 1.0 fusion.29
  128.5 5.1 %all-to-all-done.2 = bf16[128,8,256]{2,1,0:T(8,128)(2,1)S(1)} async-done(((bf16[128,8,256]{2,1,0:T(8,128)(2,1)}), bf16[128,8,256]{2,1,0:T(8,128)(2,1)S(1)}, u32[]{:S(2)}, u32[]{:S(2)}) %all-to-all-start.2) | async-done | bytes 524320 | tf_op jit(solution)/shard_map/all_to_all | solution.py:279
  133.7 0.8 slice_bitcast_fusion
  134.7 0.8 copy.28
  135.4 0.6 reduce_sum.29
  (41 shorter events, 1.7 us)
Async XLA Ops:
  4.7 6.9 %copy-start.5 = (bf16[2048,256]{1,0:T(8,128)(2,1)}, bf16[2048,256]{1,0:T(8,128)(2,1)S(1)}, u32[]{:S(2)}) copy-start(bf16[2048,256]{1,0:T(8,128)(2,1)S(1)} %constant_dynamic-update-slice_fusion) | copy-start | bytes 3145732
  11.6 11.5 %copy-start.6 = (s32[8192]{0:T(1024)S(1)}, s32[8192]{0:T(1024)}, u32[]{:S(2)}) copy-start(s32[8192]{0:T(1024)} %param.13) | copy-start | bytes 98308
  11.6 11.6 %copy-start.7 = (s32[8192]{0:T(1024)S(1)}, s32[8192]{0:T(1024)}, u32[]{:S(2)}) copy-start(s32[8192]{0:T(1024)} %param.14) | copy-start | bytes 98308
  11.6 18.8 %copy-start.1 = (bf16[256,128]{1,0:T(8,128)(2,1)S(1)}, bf16[256,128]{1,0:T(8,128)(2,1)}, u32[]{:S(2)}) copy-start(bf16[256,128]{1,0:T(8,128)(2,1)} %w2_ref.1) | copy-start | bytes 196612
  11.6 18.9 %copy-start = (bf16[384,256]{1,0:T(8,128)(2,1)S(1)}, bf16[384,256]{1,0:T(8,128)(2,1)}, u32[]{:S(2)}) copy-start(bf16[384,256]{1,0:T(8,128)(2,1)} %w1_ref.1) | copy-start | bytes 589828
  11.6 41.2 %all-to-all-start = ((bf16[128,32,256]{2,1,0:T(8,128)(2,1)}), bf16[128,32,256]{2,1,0:T(8,128)(2,1)S(1)}, u32[]{:S(2)}, u32[]{:S(2)}) async-start(bf16[128,32,256]{2,1,0:T(8,128)(2,1)} %bitcast.27), calls=%async_computation | async-start | bytes 4194304 | tf_op jit(solution)/shard_map/all_to_all | solution.py:256
  30.8 22.0 %copy-start.2 = (f32[256]{0:T(256)S(1)}, f32[256]{0:T(256)}, u32[]{:S(2)}) copy-start(f32[256]{0:T(256)} %param.16) | copy-start | bytes 3076
  52.8 2.2 %copy-start.4 = (bf16[8192,256]{1,0:T(8,128)(2,1)S(1)}, bf16[8192,256]{1,0:T(8,128)(2,1)}, u32[]{:S(2)}) copy-start(bf16[8192,256]{1,0:T(8,128)(2,1)} %fusion.8.own_hbm) | copy-start | bytes 12582916
  72.6 1.9 %copy-start.3 = (bf16[8192,256]{1,0:T(8,128)(2,1)}, bf16[8192,256]{1,0:T(8,128)(2,1)S(1)}, u32[]{:S(2)}) copy-start(bf16[8192,256]{1,0:T(8,128)(2,1)S(1)} %get-tuple-element.11) | copy-start | bytes 12582916
  74.6 39.9 %all-to-all-start.1 = ((bf16[128,40,256]{2,1,0:T(8,128)(2,1)}), bf16[128,40,256]{2,1,0:T(8,128)(2,1)S(1)}, u32[]{:S(2)}, u32[]{:S(2)}) async-start(bf16[128,40,256]{2,1,0:T(8,128)(2,1)} %get-tuple-element.12), calls=%async_computation.1 | async-start | bytes 5242880 | tf_op jit(solution)/shard_map/all_to_all | solution.py:267
  115.5 18.2 %all-to-all-start.2 = ((bf16[128,8,256]{2,1,0:T(8,128)(2,1)}), bf16[128,8,256]{2,1,0:T(8,128)(2,1)S(1)}, u32[]{:S(2)}, u32[]{:S(2)}) async-start(bf16[128,8,256]{2,1,0:T(8,128)(2,1)} %broadcast_in_dim.10), calls=%async_computation.2 | async-start | bytes 1048576 | tf_op jit(solution)/shard_map/all_to_all | solution.py:279
  120.2 1.6 %copy-start.8 = (f32[2048,256]{1,0:T(8,128)S(1)}, f32[2048,256]{1,0:T(8,128)}, u32[]{:S(2)}) copy-start(f32[2048,256]{1,0:T(8,128)} %fusion.10) | copy-start | bytes 6291460

commit v3 on v2

--- a/solution.py
+++ b/solution.py
@@ -9,6 +9,7 @@
 
 AXES = ("phi", "eta")
 BLOCK = 2048
+PACK = 1024
 SUPER = 2048
 CHUNK = 512
 ORDER = (3, 2, 1, 0)
@@ -38,7 +39,8 @@
     w2_ref,
     w2t_ref,
     bias_ref,
-    inner_ref,
+    inner_hbm,
+    dpre_hbm,
     out_ref,
     gbias_ref,
     total_ref,
@@ -46,7 +48,10 @@
     far2_ref,
     outer_ref,
     own_ref,
+    inner_ref,
+    dpre_ref,
     own_sem,
+    keep_sem,
 ):
     fetch = pltpu.make_async_copy(own_hbm, own_ref, own_sem)
     fetch.start()
@@ -91,6 +96,13 @@
                 lax.fori_loop(1, count_ref[part], more, 0)
 
         return carry
+
+    def keeps(step):
+        rows = pl.ds(pl.multiple_of(step * SUPER, SUPER), SUPER)
+        return (
+            pltpu.make_async_copy(inner_ref.at[rows], inner_hbm.at[rows], keep_sem.at[0, step]),
+            pltpu.make_async_copy(dpre_ref.at[rows], dpre_hbm.at[rows], keep_sem.at[1, step]),
+        )
 
     def mlp(step, carry):
         chunks = SUPER // CHUNK
@@ -119,6 +131,7 @@
             dpre = v.pop("dh") * (sig * (1.0 + pre * (1.0 - sig)))
             gbias_ref[...] += jnp.sum(dpre, axis=0, keepdims=True)
             v["dpre"] = dpre.astype(BF16)
+            dpre_ref[here(c), :] = v["dpre"]
 
         def stage2(c):
             v = state[c]
@@ -132,9 +145,9 @@
             dx = v.pop("dx")
             af = own_ref[here(c), :width].astype(F32)
             b = far2_ref[here(c), :width].astype(F32)
-            dprod = dx[:, 2 * width :]
-            inner_ref[here(c), width:] = (dx[:, :width] + dprod * b).astype(BF16)
-            outer_ref[here(c), width:] = (dx[:, width : 2 * width] + dprod * af).astype(BF16)
+            dprod = dx[:, width:]
+            inner_ref[here(c), width:] = (dprod * b).astype(BF16)
+            outer_ref[here(c), width:] = (dx[:, :width] + dprod * af).astype(BF16)
             rows1 = w1_ref.shape[0]
             grad_ref[:rows1, :] += dot_rows(v["x"], v["dpre"])
             grad_ref[rows1:, :] += dot_rows(v["dm"], v["h"])
@@ -145,6 +158,8 @@
                 c = t - s
                 if 0 <= c < chunks:
                     stages[s](c)
+        for copy in keeps(step):
+            copy.start()
         return carry
 
     def scatter(step, carry):
@@ -190,6 +205,10 @@
         return carry
 
     lax.fori_loop(0, ndev // 2, close_grad, 0, unroll=4)
+
+    for step in range(trips // SUPER):
+        for copy in keeps(step):
+            copy.wait()
 
 
 def triplets(remote, own, far, w1, bias, w2, ndev):
@@ -207,20 +226,25 @@
     row = remote.reshape(steps * parts, 1, PART)
     smem = pl.BlockSpec(memory_space=pltpu.SMEM)
     vmem = pl.BlockSpec(memory_space=pltpu.VMEM)
+    hbm = pl.BlockSpec(memory_space=pltpu.HBM)
     return pl.pallas_call(
         triplet_kernel,
-        in_specs=[smem] * 3 + [vmem, pl.BlockSpec(memory_space=pl.ANY)] + [vmem] * 6,
-        out_specs=[vmem] * 3,
+        in_specs=[smem] * 3 + [vmem, hbm] + [vmem] * 6,
+        out_specs=[hbm, hbm, vmem, vmem],
         scratch_shapes=[
             pltpu.VMEM((slots, pair), F32),
             pltpu.VMEM((rows1 + width, hid), F32),
             pltpu.VMEM((trips, pair), BF16),
             pltpu.VMEM((trips, pair), BF16),
             pltpu.VMEM((trips, pair), BF16),
+            pltpu.VMEM((trips, pair), BF16),
+            pltpu.VMEM((trips, hid), BF16),
             pltpu.SemaphoreType.DMA,
+            pltpu.SemaphoreType.DMA((2, trips // SUPER)),
         ],
         out_shape=[
-            jax.ShapeDtypeStruct((trips, pair), BF16),
+            pltpu.HBM((trips, pair), BF16),
+            pltpu.HBM((trips, hid), BF16),
             jax.ShapeDtypeStruct((ndev, slots // ndev + 8, pair), BF16),
             jax.ShapeDtypeStruct((1, hid), F32),
         ],
@@ -229,7 +253,120 @@
             flops=2 * trips * 600000, bytes_accessed=20 * 2**20, transcendentals=trips * hid
         ),
         name="triplets",
-    )(base, count, most, row, own, far, w1, w1.T, w2, w2.T, bias[None, :])
+    )(base, count, most, row, pltpu.with_memory_space_constraint(own, pltpu.HBM), far, w1, w1[width:].T, w2, w2.T, bias[None, :])
+
+
+def pack_kernel(
+    edges_ref,
+    cot_ref,
+    rows_ref,
+    count_ref,
+    table_hbm,
+    out_hbm,
+    table_ref,
+    index_ref,
+    out_ref,
+    table_sem,
+    out_sem,
+):
+    rows, width = edges_ref.shape
+    slots_per, ndev = rows_ref.shape
+    block = out_ref.shape[1]
+    group = block // slots_per
+    table_ref[:, :width] = edges_ref[...]
+    table_ref[:, width:] = cot_ref[...]
+    keep = pltpu.make_async_copy(table_ref, table_hbm, table_sem)
+    keep.start()
+    slot = lax.broadcasted_iota(jnp.int32, (slots_per, ndev), 0)
+    chosen = jnp.where(slot < count_ref[...], rows_ref[...], -1)
+    for d in range(ndev):
+        index_ref[d // group, (d % group) * slots_per : (d % group + 1) * slots_per, :] = (
+            jnp.broadcast_to(chosen[:, d : d + 1], (slots_per, 128))
+        )
+
+    def send(g):
+        start = pl.multiple_of(g * block, block)
+        return pltpu.make_async_copy(out_ref.at[g], out_hbm.at[pl.ds(start, block)], out_sem.at[g])
+
+    def body(g, carry):
+        index = index_ref[g]
+        lane = lax.broadcasted_iota(jnp.int32, index.shape, 1)
+        hot = jnp.concatenate(
+            [(index == lane + k * 128).astype(F32).astype(BF16) for k in range(rows // 128)], axis=1
+        )
+        out_ref[g] = dot(hot, table_ref[...]).astype(BF16)
+        send(g).start()
+        return carry
+
+    groups = out_ref.shape[0]
+    lax.fori_loop(0, groups, body, 0)
+    for g in range(groups):
+        send(g).wait()
+    keep.wait()
+
+
+def pack(edges, cotangent, rows_t, count):
+    rows, width = edges.shape
+    slots_per, ndev = rows_t.shape
+    slots = slots_per * ndev
+    groups = slots // PACK
+    vmem = pl.BlockSpec(memory_space=pltpu.VMEM)
+    return pl.pallas_call(
+        pack_kernel,
+        in_specs=[vmem] * 4,
+        out_specs=[pl.BlockSpec(memory_space=pltpu.HBM)] * 2,
+        out_shape=[
+            pltpu.HBM((rows, 2 * width), BF16),
+            pltpu.HBM((slots, 2 * width), BF16),
+        ],
+        scratch_shapes=[
+            pltpu.VMEM((rows, 2 * width), BF16),
+            pltpu.VMEM((groups, PACK, 128), jnp.int32),
+            pltpu.VMEM((groups, PACK, 2 * width), BF16),
+            pltpu.SemaphoreType.DMA,
+            pltpu.SemaphoreType.DMA((groups,)),
+        ],
+        compiler_params=pltpu.CompilerParams(vmem_limit_bytes=36 * 2**20),
+        cost_estimate=pl.CostEstimate(
+            flops=4 * slots * rows * width, bytes_accessed=4 * 2**20, transcendentals=0
+        ),
+        name="pack",
+    )(edges, cotangent, rows_t, count)
+
+
+def unpack_kernel(shared_ref, first_ref, bias_ref, second_ref):
+    width = shared_ref.shape[2] // 2
+    cut = first_ref.shape[0] // 8
+    for k in range(cut):
+        for c in range(2):
+            first_ref[8 * k : 8 * k + 8, c * width : (c + 1) * width] = shared_ref[
+                2 * k + c, :, :width
+            ].astype(F32)
+    rest = shared_ref.shape[0] // 2 - cut
+    for c in range(2):
+        tall = jnp.concatenate(
+            [shared_ref[2 * (cut + k) + c, :, :width].astype(F32) for k in range(rest)], axis=0
+        )
+        second_ref[c * width : (c + 1) * width, :] = tall.T
+    ends = jnp.sum(shared_ref[:, :, width:].astype(F32), axis=0)
+    for c in range(2):
+        bias_ref[:, c * width : (c + 1) * width] = ends[c : c + 1, :] + ends[c + 2 : c + 3, :]
+
+
+def unpack(shared, rows1, hid, width):
+    vmem = pl.BlockSpec(memory_space=pltpu.VMEM)
+    return pl.pallas_call(
+        unpack_kernel,
+        in_specs=[vmem],
+        out_specs=[vmem] * 3,
+        out_shape=[
+            jax.ShapeDtypeStruct((rows1, hid), F32),
+            jax.ShapeDtypeStruct((1, hid), F32),
+            jax.ShapeDtypeStruct((hid, width), F32),
+        ],
+        cost_estimate=pl.CostEstimate(flops=0, bytes_accessed=2**20, transcendentals=0),
+        name="unpack",
+    )(pltpu.with_memory_space_constraint(shared, pltpu.VMEM))
 
 
 def split(x):
@@ -249,10 +386,8 @@
     live = jnp.arange(slots_per, dtype=jnp.int32)[None, :] < send_count[0][:, None]
     chosen = jnp.where(live, send_rows[0], -1).reshape(slots)
     row_ids = jnp.arange(rows, dtype=jnp.int32)
-    table = jnp.concatenate([edges, cotangent], axis=1)
-    with jax.named_scope("pack"):
-        hot = (chosen[:, None] == row_ids[None, :]).astype(BF16)
-        outgoing = dot(hot, table).astype(BF16).reshape(ndev, slots_per, pair)
+    table, outgoing = pack(edges, cotangent, send_rows[0].T, send_count)
+    outgoing = outgoing.reshape(ndev, slots_per, pair)
     arrived = lax.all_to_all(outgoing, AXES, split_axis=0, concat_axis=0, tiled=True)
     arrived = arrived.reshape(slots, pair)
     with jax.named_scope("order"):
@@ -261,11 +396,13 @@
         inner = key - remote * rows
     with jax.named_scope("own_rows"):
         own = dot((inner[:, None] == row_ids[None, :]).astype(BF16), table).astype(BF16)
-    inner_sums, outbound, gbias = triplets(
+    kept, dpre, outbound, gbias = triplets(
         remote, own, arrived, w_first, bias_first, w_second, ndev
     )
     returned = lax.all_to_all(outbound, AXES, split_axis=0, concat_axis=0, tiled=True)
     with jax.named_scope("own_sums"):
+        d_inner = dot(dpre, w_first[:width].T) + kept[:, width:].astype(F32)
+        inner_sums = jnp.concatenate([kept[:, :width], d_inner.astype(BF16)], axis=1)
         own_sum = dot((row_ids[:, None] == inner[None, :]).astype(BF16), inner_sums)
         own_sum = lax.optimization_barrier(table.astype(F32) + own_sum)
     hid = w_first.shape[1]
@@ -281,11 +418,8 @@
         back = returned[:, :slots_per, :].reshape(slots, pair)
         far_sum = dot((row_ids[:, None] == chosen[None, :]).astype(BF16), back)
     both = (own_sum + far_sum).astype(BF16)
-    total = shared[:, :, :width].astype(F32).reshape(ndev // 2, 2, 8, width)
-    total = total.transpose(0, 2, 1, 3).reshape(ndev * 4, hid)
-    cut = w_first.shape[0]
-    grad_bias = jnp.sum(shared[:, :4, width:].astype(F32), axis=0).reshape(2, hid).sum(0)
-    return (both[:, :width], both[:, width:], total[:cut], grad_bias, total[cut:].T)
+    grad_first, grad_bias, grad_second = unpack(shared, w_first.shape[0], hid, width)
+    return (both[:, :width], both[:, width:], grad_first, grad_bias.reshape(hid), grad_second)
 
 
 def solution(mesh):

time: 137 us -> 131 us (0.956)
  Pallas kernels: 17.7 us -> 24.3 us
  matrix products: 40.4 us -> 34.5 us
  waiting for transfers between devices: 34.4 us -> 29.4 us
  local copies, waits for them, and re-layouts: 13.1 us -> 11.2 us
    pallas_call x1 -> x3, Pallas kernels: 17.7 us -> 24.3 us  [the longest x1 16.7 us: triplets(): pl.pallas_call(triplet_kernel, in_specs=[smem] * 3 + [vmem, hbm] + [vmem]...]
    dot_general x4, matrix products: 40.4 us -> 34.5 us  [dot(): return jnp.dot(a, b, preferred_element_type=F32)]
    all_to_all x1, waiting for transfers between devices: 21.3 us -> 17.4 us  [local(): lax.all_to_all(outbound, AXES, split_axis=0, concat_axis=0, tiled=True)]
    unnamed x23 -> x31, local copies, waits for them, and re-layouts: 8.41 us -> 5.02 us
    slice x1, local copies, waits for them, and re-layouts: 0.28 us -> 1.93 us  [local(): back = returned[:, :slots_per, :].reshape(slots, pair)]
  transfers between devices with their start and end apart: 3 -> 3, of which waited for: 3 -> 3; matrix products, arithmetic and copies ran while one was open for 31% -> 36% of each run, Pallas kernels for 0% -> 0%
where the time goes in v3:
time: 131 us; the launch traced here: 130 us
  matrix products  34.5 us (26%)
  waiting for transfers between devices  29.4 us (22%)
  Pallas kernels  24.3 us (19%)
  starting transfers between devices  21.9 us (17%)
  local copies, waits for them, and re-layouts  11.2 us (9%)
  other arithmetic  8.26 us (6%)
    dot_general x4, matrix products, dot(): return jnp.dot(a, b, preferred_element_type=F32)  34.5 us
    all_to_all x1, waiting for transfers between devices, local(): lax.all_to_all(outbound, AXES, split_axis=0, concat_axis=0, tiled=True)  17.4 us
    pallas_call x1, Pallas kernels, triplets(): pl.pallas_call(triplet_kernel, in_specs=[smem] * 3 + [vmem, hbm] + [vmem]...  16.7 us
    all_to_all x1, starting transfers between devices, local(): lax.all_to_all(outgoing, AXES, split_axis=0, concat_axis=0, tiled=True)  11.5 us
    all_to_all x1, waiting for transfers between devices, local(): lax.all_to_all(outgoing, AXES, split_axis=0, concat_axis=0, tiled=True)  7.53 us
    sort x1, other arithmetic, local(): key = jnp.sort(trip_remote * rows + trip_local)  6.77 us
    pallas_call x1, Pallas kernels, pack(): pl.pallas_call(pack_kernel, in_specs=[vmem] * 4, out_specs=[pl.BlockSpec(...  6.7 us
    all_to_all x1, starting transfers between devices, local(): lax.all_to_all(outbound, AXES, split_axis=0, concat_axis=0, tiled=True)  5.64 us
  transfers between devices with their start and end apart: 3, of which 3 were waited for; matrix products, arithmetic and copies ran while one was open for 36% of the time, Pallas kernels for 0%

profile of v3, /device:TPU:1, one launch (start us, length us, event | category | flops | bytes accessed | tf_op | source)
XLA Modules:
  0.0 130.5 jit_solution(17928861236244359058)
XLA Ops:
  0.6 0.7 copy-done.2
  1.4 0.7 copy-done.4
  2.0 1.0 copy-done.6
  3.1 1.0 copy-done.7
  4.1 6.7 %pack.1 = (bf16[2048,256]{1,0:T(8,128)(2,1)}, bf16[4096,256]{1,0:T(8,128)(2,1)}) custom-call(bf16[2048,128]{1,0:T(8,128)(2,1)S(1)} %copy-done.6, bf16[2048,128]{1,0:T(8,128)(2,1)S(1)} %copy-done.7, s32[32,128]{1,0:T(8,128)S(1)} %bitcast.19, s32[1,128]{1,0:T(1,128)S(1)} %copy-done.4), custom_call_target="tpu_custom_call" | custom-call | flops 4294967296 | bytes 4194304 | tf_op jit(solution)/shard_map/pack/pallas_call | solution.py:314
  10.9 11.5 %all-to-all-start = ((bf16[128,32,256]{2,1,0:T(8,128)(2,1)}), bf16[128,32,256]{2,1,0:T(8,128)(2,1)S(1)}, u32[]{:S(2)}, u32[]{:S(2)}) async-start(bf16[128,32,256]{2,1,0:T(8,128)(2,1)} %bitcast.22), calls=%async_computation | async-start | bytes 4194304 | tf_op jit(solution)/shard_map/all_to_all | solution.py:391
  22.5 6.8 %sort.15 = (s32[8192]{0:T(1024)S(1)}, s32[8192]{0:T(1024)}) sort(s32[8192]{0:T(1024)S(1)} %multiply_add_fusion, s32[8192]{0:T(1024)S(1)} %iota.15), dimensions={0}, to_apply=%region_0.1 | sort | flops 106496 | bytes 131072 | tf_op jit(solution)/shard_map/order/jit(sort)/sort | solution.py:394
  30.4 14.1 %fusion.6.own_hbm = bf16[8192,256]{1,0:T(8,128)(2,1)} fusion(bf16[2048,256]{1,0:T(8,128)(2,1)} %get-tuple-element.16, s32[8192]{0:T(1024)S(1)} %get-tuple-element.32), kind=kOutput, calls=%fused_computation.9 | convolution fusion | flops 8608808960 | bytes 5275648 | tf_op jit(solution)/shard_map/own_rows/dot_general | solution.py:23
  44.5 7.5 %all-to-all-done = bf16[128,32,256]{2,1,0:T(8,128)(2,1)S(1)} async-done(((bf16[128,32,256]{2,1,0:T(8,128)(2,1)}), bf16[128,32,256]{2,1,0:T(8,128)(2,1)S(1)}, u32[]{:S(2)}, u32[]{:S(2)}) %all-to-all-start) | async-done | bytes 2097184 | tf_op jit(solution)/shard_map/all_to_all | solution.py:391
  52.0 16.7 %triplets.1 = (bf16[8192,256]{1,0:T(8,128)(2,1)}, bf16[8192,256]{1,0:T(8,128)(2,1)}, bf16[128,40,256]{2,1,0:T(8,128)(2,1)}, f32[1,256]{1,0:T(1,128)S(1)}) custom-call(s32[32]{0:T(128)S(1)} %get-tuple-element.29.base_ref, s32[32]{0:T(128)S(1)} %get-tuple-element.28.count_ref, s32[4]{0:T(128)S(1)} %fusion.28.most_ref, s32[32,1,256]{2,1,0:T(1,128)S(1)} %bitcast.16, ...), custom_call_target="tpu_custom_call" | custom-call | flops 9830400000 | bytes 20971520 | tf_op jit(solution)/shard_map/triplets/pallas_call | solution.py:230
  68.7 5.6 %all-to-all-start.1 = ((bf16[128,40,256]{2,1,0:T(8,128)(2,1)}), bf16[128,40,256]{2,1,0:T(8,128)(2,1)}, u32[]{:S(2)}, u32[]{:S(2)}) async-start(bf16[128,40,256]{2,1,0:T(8,128)(2,1)} %get-tuple-element.21), calls=%async_computation.1 | async-start | bytes 5242880 | tf_op jit(solution)/shard_map/all_to_all | solution.py:402
  74.4 1.9 %slice.39 = bf16[8192,128]{1,0:T(8,128)(2,1)S(1)} slice(bf16[8192,256]{1,0:T(8,128)(2,1)} %get-tuple-element.19), slice={[0:8192], [0:128]} | slice | bytes 4194304 | tf_op jit(solution)/shard_map/own_sums/slice | solution.py:405
  76.3 0.9 copy-done.9
  77.2 3.0 %fusion.7 = bf16[8192,128]{1,0:T(8,128)(2,1)S(1)} fusion(bf16[8192,256]{1,0:T(8,128)(2,1)S(1)} %copy-done.9, bf16[8192,256]{1,0:T(8,128)(2,1)} %get-tuple-element.19, bf16[384,256]{1,0:T(8,128)(2,1)S(1)} %copy-done), kind=kOutput, calls=%fused_computation.11 | convolution fusion | flops 540016640 | bytes 8454144 | tf_op jit(solution)/shard_map/own_sums/dot_general | solution.py:23
  80.2 11.8 %fusion.11 = f32[2048,256]{1,0:T(8,128)} fusion(bf16[8192,128]{1,0:T(8,128)(2,1)S(1)} %fusion.7, bf16[8192,128]{1,0:T(8,128)(2,1)S(1)} %slice.39, s32[8192]{0:T(1024)S(1)} %get-tuple-element.32, bf16[2048,256]{1,0:T(8,128)(2,1)S(1)} %copy-done.12), kind=kOutput, calls=%fused_computation.15 | convolution fusion | flops 8616148992 | bytes 7372800 | tf_op jit(solution)/shard_map/own_sums/dot_general | solution.py:23
  92.0 17.4 %all-to-all-done.1 = bf16[128,40,256]{2,1,0:T(8,128)(2,1)} async-done(((bf16[128,40,256]{2,1,0:T(8,128)(2,1)}), bf16[128,40,256]{2,1,0:T(8,128)(2,1)}, u32[]{:S(2)}, u32[]{:S(2)}) %all-to-all-start.1) | async-done | bytes 2621472 | tf_op jit(solution)/shard_map/all_to_all | solution.py:402
  109.4 1.2 convert_reduce_fusion
  110.6 0.8 broadcast_in_dim.10
  111.4 4.8 %all-to-all-start.2 = ((bf16[128,8,256]{2,1,0:T(8,128)(2,1)}), bf16[128,8,256]{2,1,0:T(8,128)(2,1)S(1)}, u32[]{:S(2)}, u32[]{:S(2)}) async-start(bf16[128,8,256]{2,1,0:T(8,128)(2,1)} %broadcast_in_dim.10), calls=%async_computation.2 | async-start | bytes 1048576 | tf_op jit(solution)/shard_map/all_to_all | solution.py:416
  116.2 1.9 %slice.50 = bf16[128,32,256]{2,1,0:T(8,128)(2,1)S(1)} slice(bf16[128,40,256]{2,1,0:T(8,128)(2,1)} %all-to-all-done.1), slice={[0:128], [0:32], [0:256]} | slice | bytes 4194304 | tf_op jit(solution)/shard_map/far_sums/slice | solution.py:418
  118.4 5.7 %fusion.15 = bf16[2048,256]{1,0:T(8,128)(2,1)S(1)} fusion(f32[2048,256]{1,0:T(8,128)S(1)} %copy-done.13, bf16[4096,256]{1,0:T(8,128)(2,1)S(1)} %bitcast.23, s32[4096]{0:T(1024)S(1)} %broadcast_select_fusion), kind=kOutput, calls=%fused_computation.17 | convolution fusion | flops 4304404480 | bytes 5259264 | tf_op jit(solution)/shard_map/far_sums/dot_general | solution.py:23
  124.1 1.0 fusion.34
  125.1 4.5 %all-to-all-done.2.shared_ref = bf16[128,8,256]{2,1,0:T(8,128)(2,1)S(1)} async-done(((bf16[128,8,256]{2,1,0:T(8,128)(2,1)}), bf16[128,8,256]{2,1,0:T(8,128)(2,1)S(1)}, u32[]{:S(2)}, u32[]{:S(2)}) %all-to-all-start.2) | async-done | bytes 524320 | tf_op jit(solution)/shard_map/all_to_all | solution.py:416
  129.6 0.9 unpack.1
  (46 shorter events, 1.5 us)
Async XLA Ops:
  0.6 0.7 copy-start.2
  1.4 0.7 copy-start.4
  2.0 1.0 copy-start.6
  3.0 1.0 copy-start.7
  10.8 11.6 %copy-start.3 = (s32[1,128,32]{1,2,0:T(8,128)S(1)}, s32[1,128,32]{1,2,0:T(8,128)}, u32[]{:S(2)}) copy-start(s32[1,128,32]{1,2,0:T(8,128)} %param.11) | copy-start | bytes 49156
  10.8 11.7 %copy-start.10 = (s32[8192]{0:T(1024)S(1)}, s32[8192]{0:T(1024)}, u32[]{:S(2)}) copy-start(s32[8192]{0:T(1024)} %param.13) | copy-start | bytes 98308
  10.8 11.7 %copy-start.11 = (s32[8192]{0:T(1024)S(1)}, s32[8192]{0:T(1024)}, u32[]{:S(2)}) copy-start(s32[8192]{0:T(1024)} %param.14) | copy-start | bytes 98308
  10.8 18.8 %copy-start.5 = (s32[1,128]{1,0:T(1,128)S(1)}, s32[1,128]{1,0:T(1,128)}, u32[]{:S(2)}) copy-start(s32[1,128]{1,0:T(1,128)} %count_ref.1) | copy-start | bytes 1540
  10.8 19.2 %slice-start = ((bf16[384,256]{1,0:T(8,128)(2,1)}), bf16[256,256]{1,0:T(8,128)(2,1)S(1)}, s32[]{:S(2)}) async-start(bf16[384,256]{1,0:T(8,128)(2,1)} %w1_ref.1), calls=%async_computation.3 | async-start | bytes 262144 | tf_op jit(solution)/shard_map/slice | solution.py:256
  10.9 19.3 %copy-start.1 = (bf16[256,128]{1,0:T(8,128)(2,1)S(1)}, bf16[256,128]{1,0:T(8,128)(2,1)}, u32[]{:S(2)}) copy-start(bf16[256,128]{1,0:T(8,128)(2,1)} %w2_ref.1) | copy-start | bytes 196612
  10.9 41.2 %all-to-all-start = ((bf16[128,32,256]{2,1,0:T(8,128)(2,1)}), bf16[128,32,256]{2,1,0:T(8,128)(2,1)S(1)}, u32[]{:S(2)}, u32[]{:S(2)}) async-start(bf16[128,32,256]{2,1,0:T(8,128)(2,1)} %bitcast.22), calls=%async_computation | async-start | bytes 4194304 | tf_op jit(solution)/shard_map/all_to_all | solution.py:391
  30.4 21.6 %copy-start = (bf16[384,256]{1,0:T(8,128)(2,1)S(1)}, bf16[384,256]{1,0:T(8,128)(2,1)}, u32[]{:S(2)}) copy-start(bf16[384,256]{1,0:T(8,128)(2,1)} %w1_ref.1) | copy-start | bytes 589828
  30.4 21.6 %copy-start.8 = (f32[256]{0:T(256)S(1)}, f32[256]{0:T(256)}, u32[]{:S(2)}) copy-start(f32[256]{0:T(256)} %param.16) | copy-start | bytes 3076
  68.7 40.7 %all-to-all-start.1 = ((bf16[128,40,256]{2,1,0:T(8,128)(2,1)}), bf16[128,40,256]{2,1,0:T(8,128)(2,1)}, u32[]{:S(2)}, u32[]{:S(2)}) async-start(bf16[128,40,256]{2,1,0:T(8,128)(2,1)} %get-tuple-element.21), calls=%async_computation.1 | async-start | bytes 5242880 | tf_op jit(solution)/shard_map/all_to_all | solution.py:402
  74.4 2.8 %copy-start.9 = (bf16[8192,256]{1,0:T(8,128)(2,1)S(1)}, bf16[8192,256]{1,0:T(8,128)(2,1)}, u32[]{:S(2)}) copy-start(bf16[8192,256]{1,0:T(8,128)(2,1)} %get-tuple-element.20) | copy-start | bytes 12582916
  77.2 3.0 %copy-start.12 = (bf16[2048,256]{1,0:T(8,128)(2,1)S(1)}, bf16[2048,256]{1,0:T(8,128)(2,1)}, u32[]{:S(2)}) copy-start(bf16[2048,256]{1,0:T(8,128)(2,1)} %get-tuple-element.16) | copy-start | bytes 3145732
  111.4 18.2 %all-to-all-start.2 = ((bf16[128,8,256]{2,1,0:T(8,128)(2,1)}), bf16[128,8,256]{2,1,0:T(8,128)(2,1)S(1)}, u32[]{:S(2)}, u32[]{:S(2)}) async-start(bf16[128,8,256]{2,1,0:T(8,128)(2,1)} %broadcast_in_dim.10), calls=%async_computation.2 | async-start | bytes 1048576 | tf_op jit(solution)/shard_map/all_to_all | solution.py:416
  116.2 2.2 %copy-start.13 = (f32[2048,256]{1,0:T(8,128)S(1)}, f32[2048,256]{1,0:T(8,128)}, u32[]{:S(2)}) copy-start(f32[2048,256]{1,0:T(8,128)} %fusion.11) | copy-start | bytes 6291460

commit v4 on v3

--- a/solution.py
+++ b/solution.py
@@ -9,8 +9,9 @@
 
 AXES = ("phi", "eta")
 BLOCK = 2048
+GROUP = 16
 PACK = 1024
-SUPER = 2048
+SUPER = 4096
 CHUNK = 512
 ORDER = (3, 2, 1, 0)
 PART = 256
@@ -41,7 +42,7 @@
     bias_ref,
     inner_hbm,
     dpre_hbm,
-    out_ref,
+    out_hbm,
     gbias_ref,
     total_ref,
     grad_ref,
@@ -50,15 +51,23 @@
     own_ref,
     inner_ref,
     dpre_ref,
+    out_ref,
     own_sem,
     keep_sem,
+    out_sem,
 ):
-    fetch = pltpu.make_async_copy(own_hbm, own_ref, own_sem)
-    fetch.start()
+    trips = own_ref.shape[0]
+
+    def fetch(step):
+        rows = pl.ds(pl.multiple_of(step * SUPER, SUPER), SUPER)
+        return pltpu.make_async_copy(own_hbm.at[rows], own_ref.at[rows], own_sem.at[step])
+
+    for step in range(trips // SUPER):
+        fetch(step).start()
     width = own_ref.shape[1] // 2
     slots = far_ref.shape[0]
     parts = BLOCK // PART
-    ndev, _, pair = out_ref.shape
+    ndev = out_ref.shape[0]
     slots_per = slots // ndev
 
     total_ref[...] = jnp.zeros_like(total_ref)
@@ -105,6 +114,7 @@
         )
 
     def mlp(step, carry):
+        fetch(step).wait()
         chunks = SUPER // CHUNK
         state = [dict() for _ in range(chunks)]
 
@@ -162,7 +172,7 @@
             copy.start()
         return carry
 
-    def scatter(step, carry):
+    def scatter(step, sent):
         for j in range(parts):
             part = step * parts + j
             span, hot = window(part, 0)
@@ -180,32 +190,37 @@
 
                 lax.fori_loop(1, count_ref[part], more, 0)
 
+        steps = trips // BLOCK
+        follow = base_ref[jnp.minimum((step + 1) * parts, steps * parts - 1)]
+        ready = jnp.where(step == steps - 1, ndev // GROUP, follow // (GROUP * slots_per))
+        lax.fori_loop(sent, ready, close, 0)
+        return ready
+
+    def leave(q):
+        devices = pl.ds(q * GROUP, GROUP)
+        return pltpu.make_async_copy(out_ref.at[devices], out_hbm.at[devices], out_sem.at[q])
+
+    def close(q, carry):
+        for i in range(GROUP):
+            d = q * GROUP + i
+            sums = total_ref[pl.ds(pl.multiple_of(d * slots_per, slots_per), slots_per), :]
+            out_ref[d, :slots_per, :] = sums[:, :width].astype(BF16)
+            out_ref[d, slots_per : 2 * slots_per, :] = sums[:, width:].astype(BF16)
+        leave(q).start()
         return carry
-
-    trips = own_ref.shape[0]
-    lax.fori_loop(0, trips // BLOCK, gather, 0)
-    fetch.wait()
-    lax.fori_loop(0, trips // SUPER, mlp, 0)
-    lax.fori_loop(0, trips // BLOCK, scatter, 0)
-
-    def close(d, carry):
-        out_ref[d, :slots_per, :] = total_ref[
-            pl.ds(pl.multiple_of(d * slots_per, slots_per), slots_per), :
-        ].astype(BF16)
-        return carry
-
-    lax.fori_loop(0, ndev, close, 0, unroll=8)
 
     def close_grad(k, carry):
         for c in range(2):
             g = grad_ref[pl.ds(pl.multiple_of(k * 8, 8), 8), c * 128 : (c + 1) * 128]
-            high = g.astype(BF16)
-            low = (g - high.astype(F32)).astype(BF16)
-            out_ref[2 * k + c, slots_per:, :] = jnp.concatenate([high, low], axis=1)
+            out_ref[2 * k + c, 2 * slots_per :, :] = g.astype(BF16)
         return carry
 
+    lax.fori_loop(0, trips // BLOCK, gather, 0)
+    lax.fori_loop(0, trips // SUPER, mlp, 0)
     lax.fori_loop(0, ndev // 2, close_grad, 0, unroll=4)
-
+    lax.fori_loop(0, trips // BLOCK, scatter, 0)
+    for q in range(ndev // GROUP):
+        leave(q).wait()
     for step in range(trips // SUPER):
         for copy in keeps(step):
             copy.wait()
@@ -230,7 +245,7 @@
     return pl.pallas_call(
         triplet_kernel,
         in_specs=[smem] * 3 + [vmem, hbm] + [vmem] * 6,
-        out_specs=[hbm, hbm, vmem, vmem],
+        out_specs=[hbm, hbm, hbm, vmem],
         scratch_shapes=[
             pltpu.VMEM((slots, pair), F32),
             pltpu.VMEM((rows1 + width, hid), F32),
@@ -239,13 +254,15 @@
             pltpu.VMEM((trips, pair), BF16),
             pltpu.VMEM((trips, pair), BF16),
             pltpu.VMEM((trips, hid), BF16),
-            pltpu.SemaphoreType.DMA,
+            pltpu.VMEM((ndev, 2 * slots // ndev + 8, width), BF16),
+            pltpu.SemaphoreType.DMA((trips // SUPER,)),
             pltpu.SemaphoreType.DMA((2, trips // SUPER)),
+            pltpu.SemaphoreType.DMA((ndev // GROUP,)),
         ],
         out_shape=[
             pltpu.HBM((trips, pair), BF16),
             pltpu.HBM((trips, hid), BF16),
-            jax.ShapeDtypeStruct((ndev, slots // ndev + 8, pair), BF16),
+            pltpu.HBM((ndev, 2 * slots // ndev + 8, width), BF16),
             jax.ShapeDtypeStruct((1, hid), F32),
         ],
         compiler_params=pltpu.CompilerParams(vmem_limit_bytes=36 * 2**20),
@@ -257,32 +274,46 @@
 
 
 def pack_kernel(
-    edges_ref,
-    cot_ref,
+    edges_hbm,
+    cot_hbm,
+    rows_hbm,
+    count_hbm,
+    table_hbm,
+    out_hbm,
     rows_ref,
     count_ref,
-    table_hbm,
-    out_hbm,
     table_ref,
     index_ref,
     out_ref,
+    in_sem,
     table_sem,
     out_sem,
 ):
-    rows, width = edges_ref.shape
+    rows, width = edges_hbm.shape
+    fetches = [
+        pltpu.make_async_copy(rows_hbm, rows_ref, in_sem.at[0]),
+        pltpu.make_async_copy(count_hbm, count_ref, in_sem.at[1]),
+        pltpu.make_async_copy(edges_hbm, table_ref.at[:, pl.ds(0, width)], in_sem.at[2]),
+        pltpu.make_async_copy(cot_hbm, table_ref.at[:, pl.ds(width, width)], in_sem.at[3]),
+    ]
+    for copy in fetches:
+        copy.start()
     slots_per, ndev = rows_ref.shape
     block = out_ref.shape[1]
     group = block // slots_per
-    table_ref[:, :width] = edges_ref[...]
-    table_ref[:, width:] = cot_ref[...]
-    keep = pltpu.make_async_copy(table_ref, table_hbm, table_sem)
-    keep.start()
+    fetches[0].wait()
+    fetches[1].wait()
     slot = lax.broadcasted_iota(jnp.int32, (slots_per, ndev), 0)
     chosen = jnp.where(slot < count_ref[...], rows_ref[...], -1)
     for d in range(ndev):
         index_ref[d // group, (d % group) * slots_per : (d % group + 1) * slots_per, :] = (
             jnp.broadcast_to(chosen[:, d : d + 1], (slots_per, 128))
         )
+
+    fetches[2].wait()
+    fetches[3].wait()
+    keep = pltpu.make_async_copy(table_ref, table_hbm, table_sem)
+    keep.start()
 
     def send(g):
         start = pl.multiple_of(g * block, block)
@@ -310,19 +341,23 @@
     slots_per, ndev = rows_t.shape
     slots = slots_per * ndev
     groups = slots // PACK
-    vmem = pl.BlockSpec(memory_space=pltpu.VMEM)
+    hbm = pl.BlockSpec(memory_space=pltpu.HBM)
+    args = [pltpu.with_memory_space_constraint(v, pltpu.HBM) for v in (edges, cotangent, rows_t, count)]
     return pl.pallas_call(
         pack_kernel,
-        in_specs=[vmem] * 4,
-        out_specs=[pl.BlockSpec(memory_space=pltpu.HBM)] * 2,
+        in_specs=[hbm] * 4,
+        out_specs=[hbm] * 2,
         out_shape=[
             pltpu.HBM((rows, 2 * width), BF16),
             pltpu.HBM((slots, 2 * width), BF16),
         ],
         scratch_shapes=[
+            pltpu.VMEM((slots_per, ndev), jnp.int32),
+            pltpu.VMEM((1, ndev), jnp.int32),
             pltpu.VMEM((rows, 2 * width), BF16),
             pltpu.VMEM((groups, PACK, 128), jnp.int32),
             pltpu.VMEM((groups, PACK, 2 * width), BF16),
+            pltpu.SemaphoreType.DMA((4,)),
             pltpu.SemaphoreType.DMA,
             pltpu.SemaphoreType.DMA((groups,)),
         ],
@@ -331,7 +366,7 @@
             flops=4 * slots * rows * width, bytes_accessed=4 * 2**20, transcendentals=0
         ),
         name="pack",
-    )(edges, cotangent, rows_t, count)
+    )(*args)
 
 
 def unpack_kernel(shared_ref, first_ref, bias_ref, second_ref):
@@ -406,8 +441,7 @@
         own_sum = dot((row_ids[:, None] == inner[None, :]).astype(BF16), inner_sums)
         own_sum = lax.optimization_barrier(table.astype(F32) + own_sum)
     hid = w_first.shape[1]
-    mine = jnp.sum(returned[:, slots_per:, :].astype(F32), axis=0)
-    mine = (mine[:, :width] + mine[:, width:]).astype(BF16)
+    mine = jnp.sum(returned[:, 2 * slots_per :, :].astype(F32), axis=0).astype(BF16)
     bias_high, bias_low = split(gbias)
     ends = jnp.concatenate([bias_high, bias_low], axis=0).reshape(4, width)
     ends = jnp.pad(ends, ((0, 4), (0, 0)))
@@ -415,7 +449,9 @@
     share = jnp.broadcast_to(share[None], (ndev,) + share.shape)
     shared = lax.all_to_all(share, AXES, split_axis=0, concat_axis=0, tiled=True)
     with jax.named_scope("far_sums"):
-        back = returned[:, :slots_per, :].reshape(slots, pair)
+        back = jnp.concatenate(
+            [returned[:, :slots_per, :], returned[:, slots_per : 2 * slots_per, :]], axis=2
+        ).reshape(slots, pair)
         far_sum = dot((row_ids[:, None] == chosen[None, :]).astype(BF16), back)
     both = (own_sum + far_sum).astype(BF16)
     grad_first, grad_bias, grad_second = unpack(shared, w_first.shape[0], hid, width)

time: 131 us -> 124 us (0.947)
  local copies, waits for them, and re-layouts: 11.2 us -> 7.67 us
  waiting for transfers between devices: 29.4 us -> 26.6 us
    unnamed x31 -> x23, local copies, waits for them, and re-layouts: 5.02 us -> 1.29 us
    all_to_all x1, waiting for transfers between devices: 17.4 us -> 14.7 us  [local(): lax.all_to_all(outbound, AXES, split_axis=0, concat_axis=0, tiled=True)]
  transfers between devices with their start and end apart: 3 -> 3, of which waited for: 3 -> 3; matrix products, arithmetic and copies ran while one was open for 36% -> 39% of each run, Pallas kernels for 0% -> 0%
where the time goes in v4:
time: 124 us
  matrix products  34.5 us (28%)
  waiting for transfers between devices  26.6 us (21%)
  Pallas kernels  23.9 us (19%)
  starting transfers between devices  21.8 us (18%)
  other arithmetic  8.48 us (7%)
  local copies, waits for them, and re-layouts  7.67 us (6%)
    dot_general x4, matrix products, dot(): return jnp.dot(a, b, preferred_element_type=F32)  34.5 us
    pallas_call x1, Pallas kernels, triplets(): pl.pallas_call(triplet_kernel, in_specs=[smem] * 3 + [vmem, hbm] + [vmem]...  15.6 us
    all_to_all x1, waiting for transfers between devices, local(): lax.all_to_all(outbound, AXES, split_axis=0, concat_axis=0, tiled=True)  14.7 us
    all_to_all x1, starting transfers between devices, local(): lax.all_to_all(outgoing, AXES, split_axis=0, concat_axis=0, tiled=True)  11.5 us
    all_to_all x1, waiting for transfers between devices, local(): lax.all_to_all(outgoing, AXES, split_axis=0, concat_axis=0, tiled=True)  7.53 us
    pallas_call x1, Pallas kernels, pack(): pl.pallas_call(pack_kernel, in_specs=[hbm] * 4, out_specs=[hbm] * 2, out_...  7.39 us
    sort x1, other arithmetic, local(): key = jnp.sort(trip_remote * rows + trip_local)  6.77 us
    all_to_all x1, starting transfers between devices, local(): lax.all_to_all(outbound, AXES, split_axis=0, concat_axis=0, tiled=True)  5.64 us
  transfers between devices with their start and end apart: 3, of which 3 were waited for; matrix products, arithmetic and copies ran while one was open for 39% of the time, Pallas kernels for 0%

profile of v4, /device:TPU:1, one launch (start us, length us, event | category | flops | bytes accessed | tf_op | source)
XLA Modules:
  0.0 123.8 jit_solution(10523059817630597117)
XLA Ops:
  0.6 7.4 %pack.1 = (bf16[2048,256]{1,0:T(8,128)(2,1)}, bf16[4096,256]{1,0:T(8,128)(2,1)}) custom-call(bf16[2048,128]{1,0:T(8,128)(2,1)} %edges_hbm.1, bf16[2048,128]{1,0:T(8,128)(2,1)} %cot_hbm.1, s32[32,128]{1,0:T(8,128)} %bitcast.22, s32[1,128]{1,0:T(1,128)} %count_hbm.1), custom_call_target="tpu_custom_call" | custom-call | flops 4294967296 | bytes 4194304 | tf_op jit(solution)/shard_map/pack/pallas_call | solution.py:346
  8.1 11.5 %all-to-all-start = ((bf16[128,32,256]{2,1,0:T(8,128)(2,1)}), bf16[128,32,256]{2,1,0:T(8,128)(2,1)S(1)}, u32[]{:S(2)}, u32[]{:S(2)}) async-start(bf16[128,32,256]{2,1,0:T(8,128)(2,1)} %bitcast.20), calls=%async_computation | async-start | bytes 4194304 | tf_op jit(solution)/shard_map/all_to_all | solution.py:426
  19.8 6.8 %sort.15 = (s32[8192]{0:T(1024)S(1)}, s32[8192]{0:T(1024)}) sort(s32[8192]{0:T(1024)S(1)} %multiply_add_fusion, s32[8192]{0:T(1024)S(1)} %iota.15), dimensions={0}, to_apply=%region_0.1 | sort | flops 106496 | bytes 131072 | tf_op jit(solution)/shard_map/order/jit(sort)/sort | solution.py:429
  26.6 0.2 slice_reduce_fusion.1
  27.4 0.1 copy.20
  27.5 0.1 fusion.27.most_ref
  27.6 14.1 %fusion.6.own_hbm = bf16[8192,256]{1,0:T(8,128)(2,1)} fusion(bf16[2048,256]{1,0:T(8,128)(2,1)} %get-tuple-element.16, s32[8192]{0:T(1024)S(1)} %get-tuple-element.34), kind=kOutput, calls=%fused_computation.9 | convolution fusion | flops 8608808960 | bytes 5275648 | tf_op jit(solution)/shard_map/own_rows/dot_general | solution.py:24
  41.7 7.5 %all-to-all-done = bf16[128,32,256]{2,1,0:T(8,128)(2,1)S(1)} async-done(((bf16[128,32,256]{2,1,0:T(8,128)(2,1)}), bf16[128,32,256]{2,1,0:T(8,128)(2,1)S(1)}, u32[]{:S(2)}, u32[]{:S(2)}) %all-to-all-start) | async-done | bytes 2097184 | tf_op jit(solution)/shard_map/all_to_all | solution.py:426
  49.3 15.6 %triplets.1 = (bf16[8192,256]{1,0:T(8,128)(2,1)}, bf16[8192,256]{1,0:T(8,128)(2,1)}, bf16[128,72,128]{2,1,0:T(8,128)(2,1)}, f32[1,256]{1,0:T(1,128)S(1)}) custom-call(s32[32]{0:T(128)S(1)} %get-tuple-element.29.base_ref, s32[32]{0:T(128)S(1)} %get-tuple-element.28.count_ref, s32[4]{0:T(128)S(1)} %fusion.27.most_ref, s32[32,1,256]{2,1,0:T(1,128)S(1)} %bitcast.16, ...), custom_call_target="tpu_custom_call" | custom-call | flops 9830400000 | bytes 20971520 | tf_op jit(solution)/shard_map/triplets/pallas_call | solution.py:245
  64.9 5.6 %all-to-all-start.1 = ((bf16[128,72,128]{2,1,0:T(8,128)(2,1)}), bf16[128,72,128]{2,1,0:T(8,128)(2,1)}, u32[]{:S(2)}, u32[]{:S(2)}) async-start(bf16[128,72,128]{2,1,0:T(8,128)(2,1)} %get-tuple-element.21), calls=%async_computation.1 | async-start | bytes 4718592 | tf_op jit(solution)/shard_map/all_to_all | solution.py:437
  70.6 1.9 %slice.36 = bf16[8192,128]{1,0:T(8,128)(2,1)S(1)} slice(bf16[8192,256]{1,0:T(8,128)(2,1)} %get-tuple-element.19), slice={[0:8192], [0:128]} | slice | bytes 4194304 | tf_op jit(solution)/shard_map/own_sums/slice | solution.py:440
  72.4 0.9 copy-done.3
  73.4 3.0 %fusion.7 = bf16[8192,128]{1,0:T(8,128)(2,1)S(1)} fusion(bf16[8192,256]{1,0:T(8,128)(2,1)S(1)} %copy-done.3, bf16[8192,256]{1,0:T(8,128)(2,1)} %get-tuple-element.19, bf16[384,256]{1,0:T(8,128)(2,1)S(1)} %copy-done), kind=kOutput, calls=%fused_computation.11 | convolution fusion | flops 540016640 | bytes 8454144 | tf_op jit(solution)/shard_map/own_sums/dot_general | solution.py:24
  76.4 11.7 %fusion.11 = f32[2048,256]{1,0:T(8,128)} fusion(bf16[8192,128]{1,0:T(8,128)(2,1)S(1)} %fusion.7, bf16[8192,128]{1,0:T(8,128)(2,1)S(1)} %slice.36, s32[8192]{0:T(1024)S(1)} %get-tuple-element.34, bf16[2048,256]{1,0:T(8,128)(2,1)S(1)} %copy-done.8), kind=kOutput, calls=%fused_computation.15 | convolution fusion | flops 8616148992 | bytes 7372800 | tf_op jit(solution)/shard_map/own_sums/dot_general | solution.py:24
  88.1 14.7 %all-to-all-done.1 = bf16[128,72,128]{2,1,0:T(8,128)(2,1)} async-done(((bf16[128,72,128]{2,1,0:T(8,128)(2,1)}), bf16[128,72,128]{2,1,0:T(8,128)(2,1)}, u32[]{:S(2)}, u32[]{:S(2)}) %all-to-all-start.1) | async-done | bytes 2359328 | tf_op jit(solution)/shard_map/all_to_all | solution.py:437
  102.8 1.1 slice_reduce_fusion
  103.9 0.8 broadcast_in_dim.10
  104.8 4.6 %all-to-all-start.2 = ((bf16[128,8,256]{2,1,0:T(8,128)(2,1)}), bf16[128,8,256]{2,1,0:T(8,128)(2,1)S(1)}, u32[]{:S(2)}, u32[]{:S(2)}) async-start(bf16[128,8,256]{2,1,0:T(8,128)(2,1)} %broadcast_in_dim.10), calls=%async_computation.2 | async-start | bytes 1048576 | tf_op jit(solution)/shard_map/all_to_all | solution.py:450
  109.4 2.1 %fusion.33 = (bf16[128,32,128]{2,1,0:T(8,128)(2,1)S(1)}, bf16[128,32,128]{2,1,0:T(8,128)(2,1)S(1)}) fusion(bf16[128,72,128]{2,1,0:T(8,128)(2,1)} %all-to-all-done.1), kind=kLoop, calls=%fused_computation.71 | loop fusion | bytes 4194304 | tf_op jit(solution)/shard_map/far_sums/slice | solution.py:453
  111.5 0.3 pad_maximum_fusion
  111.8 5.7 %fusion.15 = bf16[2048,256]{1,0:T(8,128)(2,1)S(1)} fusion(f32[2048,256]{1,0:T(8,128)S(1)} %copy-done.9, bf16[4096,256]{1,0:T(8,128)(2,1)S(1)} %bitcast.21, s32[4096]{0:T(1024)S(1)} %broadcast_select_fusion), kind=kOutput, calls=%fused_computation.17 | convolution fusion | flops 4304404480 | bytes 5259264 | tf_op jit(solution)/shard_map/far_sums/dot_general | solution.py:24
  117.5 1.0 fusion.34
  118.6 4.3 %all-to-all-done.2.shared_ref = bf16[128,8,256]{2,1,0:T(8,128)(2,1)S(1)} async-done(((bf16[128,8,256]{2,1,0:T(8,128)(2,1)}), bf16[128,8,256]{2,1,0:T(8,128)(2,1)S(1)}, u32[]{:S(2)}, u32[]{:S(2)}) %all-to-all-start.2) | async-done | bytes 524320 | tf_op jit(solution)/shard_map/all_to_all | solution.py:450
  122.9 0.9 unpack.1
  (38 shorter events, 0.8 us)
Async XLA Ops:
  8.0 11.6 %copy-start.6 = (s32[1,128,32]{1,2,0:T(8,128)S(1)}, s32[1,128,32]{1,2,0:T(8,128)}, u32[]{:S(2)}) copy-start(s32[1,128,32]{1,2,0:T(8,128)} %param.11) | copy-start | bytes 49156
  8.0 11.7 %copy-start.4 = (s32[8192]{0:T(1024)S(1)}, s32[8192]{0:T(1024)}, u32[]{:S(2)}) copy-start(s32[8192]{0:T(1024)} %param.13) | copy-start | bytes 98308
  8.1 11.7 %copy-start.5 = (s32[8192]{0:T(1024)S(1)}, s32[8192]{0:T(1024)}, u32[]{:S(2)}) copy-start(s32[8192]{0:T(1024)} %param.14) | copy-start | bytes 98308
  8.1 18.8 %copy-start.7 = (s32[1,128]{1,0:T(1,128)S(1)}, s32[1,128]{1,0:T(1,128)}, u32[]{:S(2)}) copy-start(s32[1,128]{1,0:T(1,128)} %count_hbm.1) | copy-start | bytes 1540
  8.1 19.2 %slice-start = ((bf16[384,256]{1,0:T(8,128)(2,1)}), bf16[256,256]{1,0:T(8,128)(2,1)S(1)}, s32[]{:S(2)}) async-start(bf16[384,256]{1,0:T(8,128)(2,1)} %w1_ref.1), calls=%async_computation.3 | async-start | bytes 262144 | tf_op jit(solution)/shard_map/slice | solution.py:273
  8.1 19.3 %copy-start.1 = (bf16[256,128]{1,0:T(8,128)(2,1)S(1)}, bf16[256,128]{1,0:T(8,128)(2,1)}, u32[]{:S(2)}) copy-start(bf16[256,128]{1,0:T(8,128)(2,1)} %w2_ref.1) | copy-start | bytes 196612
  8.1 41.2 %all-to-all-start = ((bf16[128,32,256]{2,1,0:T(8,128)(2,1)}), bf16[128,32,256]{2,1,0:T(8,128)(2,1)S(1)}, u32[]{:S(2)}, u32[]{:S(2)}) async-start(bf16[128,32,256]{2,1,0:T(8,128)(2,1)} %bitcast.20), calls=%async_computation | async-start | bytes 4194304 | tf_op jit(solution)/shard_map/all_to_all | solution.py:426
  27.6 21.6 %copy-start = (bf16[384,256]{1,0:T(8,128)(2,1)S(1)}, bf16[384,256]{1,0:T(8,128)(2,1)}, u32[]{:S(2)}) copy-start(bf16[384,256]{1,0:T(8,128)(2,1)} %w1_ref.1) | copy-start | bytes 589828
  27.6 21.6 %copy-start.2 = (f32[256]{0:T(256)S(1)}, f32[256]{0:T(256)}, u32[]{:S(2)}) copy-start(f32[256]{0:T(256)} %param.16) | copy-start | bytes 3076
  64.9 37.9 %all-to-all-start.1 = ((bf16[128,72,128]{2,1,0:T(8,128)(2,1)}), bf16[128,72,128]{2,1,0:T(8,128)(2,1)}, u32[]{:S(2)}, u32[]{:S(2)}) async-start(bf16[128,72,128]{2,1,0:T(8,128)(2,1)} %get-tuple-element.21), calls=%async_computation.1 | async-start | bytes 4718592 | tf_op jit(solution)/shard_map/all_to_all | solution.py:437
  70.6 2.8 %copy-start.3 = (bf16[8192,256]{1,0:T(8,128)(2,1)S(1)}, bf16[8192,256]{1,0:T(8,128)(2,1)}, u32[]{:S(2)}) copy-start(bf16[8192,256]{1,0:T(8,128)(2,1)} %get-tuple-element.20) | copy-start | bytes 12582916
  73.4 3.0 %copy-start.8 = (bf16[2048,256]{1,0:T(8,128)(2,1)S(1)}, bf16[2048,256]{1,0:T(8,128)(2,1)}, u32[]{:S(2)}) copy-start(bf16[2048,256]{1,0:T(8,128)(2,1)} %get-tuple-element.16) | copy-start | bytes 3145732
  104.8 18.1 %all-to-all-start.2 = ((bf16[128,8,256]{2,1,0:T(8,128)(2,1)}), bf16[128,8,256]{2,1,0:T(8,128)(2,1)S(1)}, u32[]{:S(2)}, u32[]{:S(2)}) async-start(bf16[128,8,256]{2,1,0:T(8,128)(2,1)} %broadcast_in_dim.10), calls=%async_computation.2 | async-start | bytes 1048576 | tf_op jit(solution)/shard_map/all_to_all | solution.py:450
  109.4 2.4 %copy-start.9 = (f32[2048,256]{1,0:T(8,128)S(1)}, f32[2048,256]{1,0:T(8,128)}, u32[]{:S(2)}) copy-start(f32[2048,256]{1,0:T(8,128)} %fusion.11) | copy-start | bytes 6291460

commit v5 on v4

--- a/solution.py
+++ b/solution.py
@@ -8,9 +8,9 @@
 from jax.sharding import PartitionSpec as P
 
 AXES = ("phi", "eta")
-BLOCK = 2048
+BLOCK = 4096
 GROUP = 16
-PACK = 1024
+PACK = 512
 SUPER = 4096
 CHUNK = 512
 ORDER = (3, 2, 1, 0)
@@ -322,15 +322,20 @@
     def body(g, carry):
         index = index_ref[g]
         lane = lax.broadcasted_iota(jnp.int32, index.shape, 1)
-        hot = jnp.concatenate(
-            [(index == lane + k * 128).astype(F32).astype(BF16) for k in range(rows // 128)], axis=1
-        )
-        out_ref[g] = dot(hot, table_ref[...]).astype(BF16)
+        total = None
+        for k in range(0, rows, 256):
+            hot = jnp.concatenate(
+                [(index == lane + (k + c)).astype(F32).astype(BF16) for c in (0, 128)], axis=1
+            )
+            term = dot(hot, table_ref[k : k + 256, :])
+            total = term if total is None else total + term
+        out_ref[g] = total.astype(BF16)
         send(g).start()
         return carry
 
     groups = out_ref.shape[0]
-    lax.fori_loop(0, groups, body, 0)
+    for g in range(groups):
+        body(g, 0)
     for g in range(groups):
         send(g).wait()
     keep.wait()
@@ -370,20 +375,21 @@
 
 
 def unpack_kernel(shared_ref, first_ref, bias_ref, second_ref):
-    width = shared_ref.shape[2] // 2
+    width = shared_ref.shape[3]
     cut = first_ref.shape[0] // 8
+
+    def piece(k, c):
+        d = 2 * k + c
+        return jnp.concatenate([shared_ref[d, 0], shared_ref[d, 1]], axis=0).astype(F32)
+
     for k in range(cut):
         for c in range(2):
-            first_ref[8 * k : 8 * k + 8, c * width : (c + 1) * width] = shared_ref[
-                2 * k + c, :, :width
-            ].astype(F32)
+            first_ref[8 * k : 8 * k + 8, c * width : (c + 1) * width] = piece(k, c)
     rest = shared_ref.shape[0] // 2 - cut
     for c in range(2):
-        tall = jnp.concatenate(
-            [shared_ref[2 * (cut + k) + c, :, :width].astype(F32) for k in range(rest)], axis=0
-        )
+        tall = jnp.concatenate([piece(cut + k, c) for k in range(rest)], axis=0)
         second_ref[c * width : (c + 1) * width, :] = tall.T
-    ends = jnp.sum(shared_ref[:, :, width:].astype(F32), axis=0)
+    ends = jnp.sum(shared_ref[:, 2].astype(F32), axis=0)
     for c in range(2):
         bias_ref[:, c * width : (c + 1) * width] = ends[c : c + 1, :] + ends[c + 2 : c + 3, :]
 
@@ -443,9 +449,8 @@
     hid = w_first.shape[1]
     mine = jnp.sum(returned[:, 2 * slots_per :, :].astype(F32), axis=0).astype(BF16)
     bias_high, bias_low = split(gbias)
-    ends = jnp.concatenate([bias_high, bias_low], axis=0).reshape(4, width)
-    ends = jnp.pad(ends, ((0, 4), (0, 0)))
-    share = jnp.concatenate([mine, ends], axis=1)
+    ends = jnp.concatenate([bias_high, bias_low], axis=0).reshape(1, 4, width)
+    share = jnp.concatenate([mine.reshape(2, 4, width), ends], axis=0)
     share = jnp.broadcast_to(share[None], (ndev,) + share.shape)
     shared = lax.all_to_all(share, AXES, split_axis=0, concat_axis=0, tiled=True)
     with jax.named_scope("far_sums"):

time: 124 us -> 122 us (0.984)
  waiting for transfers between devices: 26.6 us -> 25.3 us
    all_to_all x1, waiting for transfers between devices: 4.29 us -> 3.02 us  [local(): lax.all_to_all(share, AXES, split_axis=0, concat_axis=0, tiled=True)]
where the time goes in v5:
time: 122 us
  matrix products  34.5 us (28%)
  waiting for transfers between devices  25.3 us (21%)
  Pallas kernels  23 us (19%)
  starting transfers between devices  21.7 us (18%)
  other arithmetic  8.48 us (7%)
  local copies, waits for them, and re-layouts  7.68 us (6%)
    dot_general x4, matrix products, dot(): return jnp.dot(a, b, preferred_element_type=F32)  34.5 us
    pallas_call x1, Pallas kernels, triplets(): pl.pallas_call(triplet_kernel, in_specs=[smem] * 3 + [vmem, hbm] + [vmem]...  15 us
    all_to_all x1, waiting for transfers between devices, local(): lax.all_to_all(outbound, AXES, split_axis=0, concat_axis=0, tiled=True)  14.7 us
    all_to_all x1, starting transfers between devices, local(): lax.all_to_all(outgoing, AXES, split_axis=0, concat_axis=0, tiled=True)  11.5 us
    all_to_all x1, waiting for transfers between devices, local(): lax.all_to_all(outgoing, AXES, split_axis=0, concat_axis=0, tiled=True)  7.53 us
    pallas_call x1, Pallas kernels, pack(): pl.pallas_call(pack_kernel, in_specs=[hbm] * 4, out_specs=[hbm] * 2, out_...  7.04 us
    sort x1, other arithmetic, local(): key = jnp.sort(trip_remote * rows + trip_local)  6.77 us
    all_to_all x1, starting transfers between devices, local(): lax.all_to_all(outbound, AXES, split_axis=0, concat_axis=0, tiled=True)  5.61 us
  transfers between devices with their start and end apart: 3, of which 3 were waited for; matrix products, arithmetic and copies ran while one was open for 39% of the time, Pallas kernels for 0%

profile of v5, /device:TPU:1, one launch (start us, length us, event | category | flops | bytes accessed | tf_op | source)
XLA Modules:
  0.0 121.5 jit_solution(9333339342044406180)
XLA Ops:
  0.6 7.0 %pack.1 = (bf16[2048,256]{1,0:T(8,128)(2,1)}, bf16[4096,256]{1,0:T(8,128)(2,1)}) custom-call(bf16[2048,128]{1,0:T(8,128)(2,1)} %edges_hbm.1, bf16[2048,128]{1,0:T(8,128)(2,1)} %cot_hbm.1, s32[32,128]{1,0:T(8,128)} %bitcast.23, s32[1,128]{1,0:T(1,128)} %count_hbm.1), custom_call_target="tpu_custom_call" | custom-call | flops 4294967296 | bytes 4194304 | tf_op jit(solution)/shard_map/pack/pallas_call | solution.py:351
  7.8 11.5 %all-to-all-start = ((bf16[128,32,256]{2,1,0:T(8,128)(2,1)}), bf16[128,32,256]{2,1,0:T(8,128)(2,1)S(1)}, u32[]{:S(2)}, u32[]{:S(2)}) async-start(bf16[128,32,256]{2,1,0:T(8,128)(2,1)} %bitcast.21), calls=%async_computation | async-start | bytes 4194304 | tf_op jit(solution)/shard_map/all_to_all | solution.py:432
  19.4 6.8 %sort.15 = (s32[8192]{0:T(1024)S(1)}, s32[8192]{0:T(1024)}) sort(s32[8192]{0:T(1024)S(1)} %multiply_add_fusion, s32[8192]{0:T(1024)S(1)} %iota.15), dimensions={0}, to_apply=%region_0.1 | sort | flops 106496 | bytes 131072 | tf_op jit(solution)/shard_map/order/jit(sort)/sort | solution.py:435
  26.2 0.2 slice_reduce_fusion.1
  27.0 0.1 copy.20
  27.1 0.1 add_reduce_fusion.most_ref
  27.3 14.1 %fusion.6.own_hbm = bf16[8192,256]{1,0:T(8,128)(2,1)} fusion(bf16[2048,256]{1,0:T(8,128)(2,1)} %get-tuple-element.16, s32[8192]{0:T(1024)S(1)} %get-tuple-element.34), kind=kOutput, calls=%fused_computation.9 | convolution fusion | flops 8608808960 | bytes 5275648 | tf_op jit(solution)/shard_map/own_rows/dot_general | solution.py:24
  41.4 7.5 %all-to-all-done = bf16[128,32,256]{2,1,0:T(8,128)(2,1)S(1)} async-done(((bf16[128,32,256]{2,1,0:T(8,128)(2,1)}), bf16[128,32,256]{2,1,0:T(8,128)(2,1)S(1)}, u32[]{:S(2)}, u32[]{:S(2)}) %all-to-all-start) | async-done | bytes 2097184 | tf_op jit(solution)/shard_map/all_to_all | solution.py:432
  48.9 15.0 %triplets.1 = (bf16[8192,256]{1,0:T(8,128)(2,1)}, bf16[8192,256]{1,0:T(8,128)(2,1)}, bf16[128,72,128]{2,1,0:T(8,128)(2,1)}, f32[1,256]{1,0:T(1,128)S(1)}) custom-call(s32[32]{0:T(128)S(1)} %get-tuple-element.29.base_ref, s32[32]{0:T(128)S(1)} %get-tuple-element.28.count_ref, s32[2]{0:T(128)S(1)} %add_reduce_fusion.most_ref, s32[32,1,256]{2,1,0:T(1,128)S(1)} %bitcast.17, ...), custom_call_target="tpu_custom_call" | custom-call | flops 9830400000 | bytes 20971520 | tf_op jit(solution)/shard_map/triplets/pallas_call | solution.py:245
  63.9 5.6 %all-to-all-start.1 = ((bf16[128,72,128]{2,1,0:T(8,128)(2,1)}), bf16[128,72,128]{2,1,0:T(8,128)(2,1)}, u32[]{:S(2)}, u32[]{:S(2)}) async-start(bf16[128,72,128]{2,1,0:T(8,128)(2,1)} %get-tuple-element.21), calls=%async_computation.1 | async-start | bytes 4718592 | tf_op jit(solution)/shard_map/all_to_all | solution.py:443
  69.5 1.9 %slice.36 = bf16[8192,128]{1,0:T(8,128)(2,1)S(1)} slice(bf16[8192,256]{1,0:T(8,128)(2,1)} %get-tuple-element.19), slice={[0:8192], [0:128]} | slice | bytes 4194304 | tf_op jit(solution)/shard_map/own_sums/slice | solution.py:446
  71.4 0.9 copy-done.3
  72.4 3.0 %fusion.7 = bf16[8192,128]{1,0:T(8,128)(2,1)S(1)} fusion(bf16[8192,256]{1,0:T(8,128)(2,1)S(1)} %copy-done.3, bf16[8192,256]{1,0:T(8,128)(2,1)} %get-tuple-element.19, bf16[384,256]{1,0:T(8,128)(2,1)S(1)} %copy-done), kind=kOutput, calls=%fused_computation.11 | convolution fusion | flops 540016640 | bytes 8454144 | tf_op jit(solution)/shard_map/own_sums/dot_general | solution.py:24
  75.3 11.7 %fusion.11 = f32[2048,256]{1,0:T(8,128)} fusion(bf16[8192,128]{1,0:T(8,128)(2,1)S(1)} %fusion.7, bf16[8192,128]{1,0:T(8,128)(2,1)S(1)} %slice.36, s32[8192]{0:T(1024)S(1)} %get-tuple-element.34, bf16[2048,256]{1,0:T(8,128)(2,1)S(1)} %copy-done.8), kind=kOutput, calls=%fused_computation.15 | convolution fusion | flops 8616148992 | bytes 7372800 | tf_op jit(solution)/shard_map/own_sums/dot_general | solution.py:24
  87.1 14.7 %all-to-all-done.1 = bf16[128,72,128]{2,1,0:T(8,128)(2,1)} async-done(((bf16[128,72,128]{2,1,0:T(8,128)(2,1)}), bf16[128,72,128]{2,1,0:T(8,128)(2,1)}, u32[]{:S(2)}, u32[]{:S(2)}) %all-to-all-start.1) | async-done | bytes 2359328 | tf_op jit(solution)/shard_map/all_to_all | solution.py:443
  101.8 1.1 slice_reduce_fusion
  102.9 0.9 broadcast_in_dim.10
  103.8 4.6 %all-to-all-start.2 = ((bf16[128,3,4,128]{3,2,1,0:T(4,128)(2,1)}), bf16[128,3,4,128]{3,2,1,0:T(4,128)(2,1)S(1)}, u32[]{:S(2)}, u32[]{:S(2)}) async-start(bf16[128,3,4,128]{3,2,1,0:T(4,128)(2,1)} %broadcast_in_dim.10), calls=%async_computation.2 | async-start | bytes 786432 | tf_op jit(solution)/shard_map/all_to_all | solution.py:455
  108.4 2.1 %fusion.22 = (bf16[128,32,128]{2,1,0:T(8,128)(2,1)S(1)}, bf16[128,32,128]{2,1,0:T(8,128)(2,1)S(1)}) fusion(bf16[128,72,128]{2,1,0:T(8,128)(2,1)} %all-to-all-done.1), kind=kLoop, calls=%fused_computation.59 | loop fusion | bytes 4194304 | tf_op jit(solution)/shard_map/far_sums/slice | solution.py:458
  110.5 0.3 pad_maximum_fusion
  110.8 5.7 %fusion.15 = bf16[2048,256]{1,0:T(8,128)(2,1)S(1)} fusion(f32[2048,256]{1,0:T(8,128)S(1)} %copy-done.9, bf16[4096,256]{1,0:T(8,128)(2,1)S(1)} %bitcast.22, s32[4096]{0:T(1024)S(1)} %broadcast_select_fusion), kind=kOutput, calls=%fused_computation.17 | convolution fusion | flops 4304404480 | bytes 5259264 | tf_op jit(solution)/shard_map/far_sums/dot_general | solution.py:24
  116.5 1.0 fusion.23
  117.5 3.0 %all-to-all-done.2.shared_ref = bf16[128,3,4,128]{3,2,1,0:T(4,128)(2,1)S(1)} async-done(((bf16[128,3,4,128]{3,2,1,0:T(4,128)(2,1)}), bf16[128,3,4,128]{3,2,1,0:T(4,128)(2,1)S(1)}, u32[]{:S(2)}, u32[]{:S(2)}) %all-to-all-start.2) | async-done | bytes 393248 | tf_op jit(solution)/shard_map/all_to_all | solution.py:455
  120.6 1.0 unpack.1
  (38 shorter events, 0.8 us)
Async XLA Ops:
  7.7 11.6 %copy-start.6 = (s32[1,128,32]{1,2,0:T(8,128)S(1)}, s32[1,128,32]{1,2,0:T(8,128)}, u32[]{:S(2)}) copy-start(s32[1,128,32]{1,2,0:T(8,128)} %param.11) | copy-start | bytes 49156
  7.7 11.7 %copy-start.4 = (s32[8192]{0:T(1024)S(1)}, s32[8192]{0:T(1024)}, u32[]{:S(2)}) copy-start(s32[8192]{0:T(1024)} %param.13) | copy-start | bytes 98308
  7.7 11.7 %copy-start.5 = (s32[8192]{0:T(1024)S(1)}, s32[8192]{0:T(1024)}, u32[]{:S(2)}) copy-start(s32[8192]{0:T(1024)} %param.14) | copy-start | bytes 98308
  7.7 18.8 %copy-start.7 = (s32[1,128]{1,0:T(1,128)S(1)}, s32[1,128]{1,0:T(1,128)}, u32[]{:S(2)}) copy-start(s32[1,128]{1,0:T(1,128)} %count_hbm.1) | copy-start | bytes 1540
  7.7 19.2 %slice-start = ((bf16[384,256]{1,0:T(8,128)(2,1)}), bf16[256,256]{1,0:T(8,128)(2,1)S(1)}, s32[]{:S(2)}) async-start(bf16[384,256]{1,0:T(8,128)(2,1)} %w1_ref.1), calls=%async_computation.3 | async-start | bytes 262144 | tf_op jit(solution)/shard_map/slice | solution.py:273
  7.7 19.3 %copy-start.1 = (bf16[256,128]{1,0:T(8,128)(2,1)S(1)}, bf16[256,128]{1,0:T(8,128)(2,1)}, u32[]{:S(2)}) copy-start(bf16[256,128]{1,0:T(8,128)(2,1)} %w2_ref.1) | copy-start | bytes 196612
  7.8 41.2 %all-to-all-start = ((bf16[128,32,256]{2,1,0:T(8,128)(2,1)}), bf16[128,32,256]{2,1,0:T(8,128)(2,1)S(1)}, u32[]{:S(2)}, u32[]{:S(2)}) async-start(bf16[128,32,256]{2,1,0:T(8,128)(2,1)} %bitcast.21), calls=%async_computation | async-start | bytes 4194304 | tf_op jit(solution)/shard_map/all_to_all | solution.py:432
  27.3 21.6 %copy-start = (bf16[384,256]{1,0:T(8,128)(2,1)S(1)}, bf16[384,256]{1,0:T(8,128)(2,1)}, u32[]{:S(2)}) copy-start(bf16[384,256]{1,0:T(8,128)(2,1)} %w1_ref.1) | copy-start | bytes 589828
  27.3 21.6 %copy-start.2 = (f32[256]{0:T(256)S(1)}, f32[256]{0:T(256)}, u32[]{:S(2)}) copy-start(f32[256]{0:T(256)} %param.16) | copy-start | bytes 3076
  63.9 37.9 %all-to-all-start.1 = ((bf16[128,72,128]{2,1,0:T(8,128)(2,1)}), bf16[128,72,128]{2,1,0:T(8,128)(2,1)}, u32[]{:S(2)}, u32[]{:S(2)}) async-start(bf16[128,72,128]{2,1,0:T(8,128)(2,1)} %get-tuple-element.21), calls=%async_computation.1 | async-start | bytes 4718592 | tf_op jit(solution)/shard_map/all_to_all | solution.py:443
  69.5 2.8 %copy-start.3 = (bf16[8192,256]{1,0:T(8,128)(2,1)S(1)}, bf16[8192,256]{1,0:T(8,128)(2,1)}, u32[]{:S(2)}) copy-start(bf16[8192,256]{1,0:T(8,128)(2,1)} %get-tuple-element.20) | copy-start | bytes 12582916
  72.4 3.0 %copy-start.8 = (bf16[2048,256]{1,0:T(8,128)(2,1)S(1)}, bf16[2048,256]{1,0:T(8,128)(2,1)}, u32[]{:S(2)}) copy-start(bf16[2048,256]{1,0:T(8,128)(2,1)} %get-tuple-element.16) | copy-start | bytes 3145732
  103.8 16.8 %all-to-all-start.2 = ((bf16[128,3,4,128]{3,2,1,0:T(4,128)(2,1)}), bf16[128,3,4,128]{3,2,1,0:T(4,128)(2,1)S(1)}, u32[]{:S(2)}, u32[]{:S(2)}) async-start(bf16[128,3,4,128]{3,2,1,0:T(4,128)(2,1)} %broadcast_in_dim.10), calls=%async_computation.2 | async-start | bytes 786432 | tf_op jit(solution)/shard_map/all_to_all | solution.py:455
  108.4 2.4 %copy-start.9 = (f32[2048,256]{1,0:T(8,128)S(1)}, f32[2048,256]{1,0:T(8,128)}, u32[]{:S(2)}) copy-start(f32[2048,256]{1,0:T(8,128)} %fusion.11) | copy-start | bytes 6291460

commit v6 on v5

--- a/solution.py
+++ b/solution.py
@@ -70,7 +70,6 @@
     ndev = out_ref.shape[0]
     slots_per = slots // ndev
 
-    total_ref[...] = jnp.zeros_like(total_ref)
     grad_ref[...] = jnp.zeros_like(grad_ref)
     gbias_ref[...] = jnp.zeros_like(gbias_ref)
 
@@ -86,11 +85,15 @@
     def place(part):
         return pl.ds(pl.multiple_of(part * PART, PART), PART)
 
+    zone = slots * PART // trips
+
     def gather(step, carry):
         for j in range(parts):
             part = step * parts + j
             span, hot = window(part, 0)
             far2_ref[place(part), :] = dot_rows(hot, far_ref[span, :]).astype(BF16)
+            blank = pl.ds(pl.multiple_of(part * zone, zone), zone)
+            total_ref[blank, :] = jnp.zeros((zone, 2 * width), F32)
 
         @pl.when(most_ref[step] > 1)
         def _():
@@ -149,6 +152,9 @@
             inner_ref[here(c), :width] = mb
             outer_ref[here(c), :width] = mb
             v["dx"] = dot(v["dpre"], w1t_ref[...])
+            rows1 = w1_ref.shape[0]
+            grad_ref[:rows1, :] += dot_rows(v["x"], v["dpre"])
+            grad_ref[rows1:, :] += dot_rows(v["dm"], v["h"])
 
         def stage3(c):
             v = state[c]
@@ -158,9 +164,6 @@
             dprod = dx[:, width:]
             inner_ref[here(c), width:] = (dprod * b).astype(BF16)
             outer_ref[here(c), width:] = (dx[:, :width] + dprod * af).astype(BF16)
-            rows1 = w1_ref.shape[0]
-            grad_ref[:rows1, :] += dot_rows(v["x"], v["dpre"])
-            grad_ref[rows1:, :] += dot_rows(v["dm"], v["h"])
 
         stages = [stage0, stage1, stage2, stage3]
         for t in range(chunks + len(stages) - 1):

time: 122 us -> 121 us (level)
  no operation moved by 1% of the time
where the time goes in v6:
time: 121 us
  matrix products  34.5 us (29%)
  waiting for transfers between devices  25.3 us (21%)
  Pallas kernels  22.4 us (19%)
  starting transfers between devices  21.8 us (18%)
  other arithmetic  8.48 us (7%)
  local copies, waits for them, and re-layouts  7.68 us (6%)
    dot_general x4, matrix products, dot(): return jnp.dot(a, b, preferred_element_type=F32)  34.5 us
    all_to_all x1, waiting for transfers between devices, local(): lax.all_to_all(outbound, AXES, split_axis=0, concat_axis=0, tiled=True)  14.7 us
    pallas_call x1, Pallas kernels, triplets(): pl.pallas_call(triplet_kernel, in_specs=[smem] * 3 + [vmem, hbm] + [vmem]...  14.4 us
    all_to_all x1, starting transfers between devices, local(): lax.all_to_all(outgoing, AXES, split_axis=0, concat_axis=0, tiled=True)  11.5 us
    all_to_all x1, waiting for transfers between devices, local(): lax.all_to_all(outgoing, AXES, split_axis=0, concat_axis=0, tiled=True)  7.53 us
    pallas_call x1, Pallas kernels, pack(): pl.pallas_call(pack_kernel, in_specs=[hbm] * 4, out_specs=[hbm] * 2, out_...  7.04 us
    sort x1, other arithmetic, local(): key = jnp.sort(trip_remote * rows + trip_local)  6.77 us
    all_to_all x1, starting transfers between devices, local(): lax.all_to_all(outbound, AXES, split_axis=0, concat_axis=0, tiled=True)  5.66 us
  transfers between devices with their start and end apart: 3, of which 3 were waited for; matrix products, arithmetic and copies ran while one was open for 39% of the time, Pallas kernels for 0%

profile of v6, /device:TPU:1, one launch (start us, length us, event | category | flops | bytes accessed | tf_op | source)
XLA Modules:
  0.0 121.0 jit_solution(8321836347572859066)
XLA Ops:
  0.6 7.0 %pack.1 = (bf16[2048,256]{1,0:T(8,128)(2,1)}, bf16[4096,256]{1,0:T(8,128)(2,1)}) custom-call(bf16[2048,128]{1,0:T(8,128)(2,1)} %edges_hbm.1, bf16[2048,128]{1,0:T(8,128)(2,1)} %cot_hbm.1, s32[32,128]{1,0:T(8,128)} %bitcast.23, s32[1,128]{1,0:T(1,128)} %count_hbm.1), custom_call_target="tpu_custom_call" | custom-call | flops 4294967296 | bytes 4194304 | tf_op jit(solution)/shard_map/pack/pallas_call | solution.py:354
  7.8 11.5 %all-to-all-start = ((bf16[128,32,256]{2,1,0:T(8,128)(2,1)}), bf16[128,32,256]{2,1,0:T(8,128)(2,1)S(1)}, u32[]{:S(2)}, u32[]{:S(2)}) async-start(bf16[128,32,256]{2,1,0:T(8,128)(2,1)} %bitcast.21), calls=%async_computation | async-start | bytes 4194304 | tf_op jit(solution)/shard_map/all_to_all | solution.py:435
  19.4 6.8 %sort.15 = (s32[8192]{0:T(1024)S(1)}, s32[8192]{0:T(1024)}) sort(s32[8192]{0:T(1024)S(1)} %multiply_add_fusion, s32[8192]{0:T(1024)S(1)} %iota.15), dimensions={0}, to_apply=%region_0.1 | sort | flops 106496 | bytes 131072 | tf_op jit(solution)/shard_map/order/jit(sort)/sort | solution.py:438
  26.2 0.2 slice_reduce_fusion.1
  27.0 0.1 copy.20
  27.1 0.1 add_reduce_fusion.most_ref
  27.3 14.1 %fusion.6.own_hbm = bf16[8192,256]{1,0:T(8,128)(2,1)} fusion(bf16[2048,256]{1,0:T(8,128)(2,1)} %get-tuple-element.16, s32[8192]{0:T(1024)S(1)} %get-tuple-element.34), kind=kOutput, calls=%fused_computation.9 | convolution fusion | flops 8608808960 | bytes 5275648 | tf_op jit(solution)/shard_map/own_rows/dot_general | solution.py:24
  41.4 7.5 %all-to-all-done = bf16[128,32,256]{2,1,0:T(8,128)(2,1)S(1)} async-done(((bf16[128,32,256]{2,1,0:T(8,128)(2,1)}), bf16[128,32,256]{2,1,0:T(8,128)(2,1)S(1)}, u32[]{:S(2)}, u32[]{:S(2)}) %all-to-all-start) | async-done | bytes 2097184 | tf_op jit(solution)/shard_map/all_to_all | solution.py:435
  48.9 14.4 %triplets.1 = (bf16[8192,256]{1,0:T(8,128)(2,1)}, bf16[8192,256]{1,0:T(8,128)(2,1)}, bf16[128,72,128]{2,1,0:T(8,128)(2,1)}, f32[1,256]{1,0:T(1,128)S(1)}) custom-call(s32[32]{0:T(128)S(1)} %get-tuple-element.29.base_ref, s32[32]{0:T(128)S(1)} %get-tuple-element.28.count_ref, s32[2]{0:T(128)S(1)} %add_reduce_fusion.most_ref, s32[32,1,256]{2,1,0:T(1,128)S(1)} %bitcast.17, ...), custom_call_target="tpu_custom_call" | custom-call | flops 9830400000 | bytes 20971520 | tf_op jit(solution)/shard_map/triplets/pallas_call | solution.py:248
  63.4 5.7 %all-to-all-start.1 = ((bf16[128,72,128]{2,1,0:T(8,128)(2,1)}), bf16[128,72,128]{2,1,0:T(8,128)(2,1)}, u32[]{:S(2)}, u32[]{:S(2)}) async-start(bf16[128,72,128]{2,1,0:T(8,128)(2,1)} %get-tuple-element.21), calls=%async_computation.1 | async-start | bytes 4718592 | tf_op jit(solution)/shard_map/all_to_all | solution.py:446
  69.0 1.9 %slice.36 = bf16[8192,128]{1,0:T(8,128)(2,1)S(1)} slice(bf16[8192,256]{1,0:T(8,128)(2,1)} %get-tuple-element.19), slice={[0:8192], [0:128]} | slice | bytes 4194304 | tf_op jit(solution)/shard_map/own_sums/slice | solution.py:449
  70.9 0.9 copy-done.3
  71.8 3.0 %fusion.7 = bf16[8192,128]{1,0:T(8,128)(2,1)S(1)} fusion(bf16[8192,256]{1,0:T(8,128)(2,1)S(1)} %copy-done.3, bf16[8192,256]{1,0:T(8,128)(2,1)} %get-tuple-element.19, bf16[384,256]{1,0:T(8,128)(2,1)S(1)} %copy-done), kind=kOutput, calls=%fused_computation.11 | convolution fusion | flops 540016640 | bytes 8454144 | tf_op jit(solution)/shard_map/own_sums/dot_general | solution.py:24
  74.8 11.7 %fusion.11 = f32[2048,256]{1,0:T(8,128)} fusion(bf16[8192,128]{1,0:T(8,128)(2,1)S(1)} %fusion.7, bf16[8192,128]{1,0:T(8,128)(2,1)S(1)} %slice.36, s32[8192]{0:T(1024)S(1)} %get-tuple-element.34, bf16[2048,256]{1,0:T(8,128)(2,1)S(1)} %copy-done.8), kind=kOutput, calls=%fused_computation.15 | convolution fusion | flops 8616148992 | bytes 7372800 | tf_op jit(solution)/shard_map/own_sums/dot_general | solution.py:24
  86.6 14.7 %all-to-all-done.1 = bf16[128,72,128]{2,1,0:T(8,128)(2,1)} async-done(((bf16[128,72,128]{2,1,0:T(8,128)(2,1)}), bf16[128,72,128]{2,1,0:T(8,128)(2,1)}, u32[]{:S(2)}, u32[]{:S(2)}) %all-to-all-start.1) | async-done | bytes 2359328 | tf_op jit(solution)/shard_map/all_to_all | solution.py:446
  101.3 1.1 slice_reduce_fusion
  102.4 0.9 broadcast_in_dim.10
  103.2 4.6 %all-to-all-start.2 = ((bf16[128,3,4,128]{3,2,1,0:T(4,128)(2,1)}), bf16[128,3,4,128]{3,2,1,0:T(4,128)(2,1)S(1)}, u32[]{:S(2)}, u32[]{:S(2)}) async-start(bf16[128,3,4,128]{3,2,1,0:T(4,128)(2,1)} %broadcast_in_dim.10), calls=%async_computation.2 | async-start | bytes 786432 | tf_op jit(solution)/shard_map/all_to_all | solution.py:458
  107.9 2.1 %fusion.22 = (bf16[128,32,128]{2,1,0:T(8,128)(2,1)S(1)}, bf16[128,32,128]{2,1,0:T(8,128)(2,1)S(1)}) fusion(bf16[128,72,128]{2,1,0:T(8,128)(2,1)} %all-to-all-done.1), kind=kLoop, calls=%fused_computation.59 | loop fusion | bytes 4194304 | tf_op jit(solution)/shard_map/far_sums/slice | solution.py:461
  110.0 0.3 pad_maximum_fusion
  110.3 5.7 %fusion.15 = bf16[2048,256]{1,0:T(8,128)(2,1)S(1)} fusion(f32[2048,256]{1,0:T(8,128)S(1)} %copy-done.9, bf16[4096,256]{1,0:T(8,128)(2,1)S(1)} %bitcast.22, s32[4096]{0:T(1024)S(1)} %broadcast_select_fusion), kind=kOutput, calls=%fused_computation.17 | convolution fusion | flops 4304404480 | bytes 5259264 | tf_op jit(solution)/shard_map/far_sums/dot_general | solution.py:24
  116.0 1.0 fusion.23
  117.0 3.0 %all-to-all-done.2.shared_ref = bf16[128,3,4,128]{3,2,1,0:T(4,128)(2,1)S(1)} async-done(((bf16[128,3,4,128]{3,2,1,0:T(4,128)(2,1)}), bf16[128,3,4,128]{3,2,1,0:T(4,128)(2,1)S(1)}, u32[]{:S(2)}, u32[]{:S(2)}) %all-to-all-start.2) | async-done | bytes 393248 | tf_op jit(solution)/shard_map/all_to_all | solution.py:458
  120.0 1.0 unpack.1
  (38 shorter events, 0.8 us)
Async XLA Ops:
  7.7 11.6 %copy-start.6 = (s32[1,128,32]{1,2,0:T(8,128)S(1)}, s32[1,128,32]{1,2,0:T(8,128)}, u32[]{:S(2)}) copy-start(s32[1,128,32]{1,2,0:T(8,128)} %param.11) | copy-start | bytes 49156
  7.7 11.7 %copy-start.4 = (s32[8192]{0:T(1024)S(1)}, s32[8192]{0:T(1024)}, u32[]{:S(2)}) copy-start(s32[8192]{0:T(1024)} %param.13) | copy-start | bytes 98308
  7.7 11.7 %copy-start.5 = (s32[8192]{0:T(1024)S(1)}, s32[8192]{0:T(1024)}, u32[]{:S(2)}) copy-start(s32[8192]{0:T(1024)} %param.14) | copy-start | bytes 98308
  7.7 18.8 %copy-start.7 = (s32[1,128]{1,0:T(1,128)S(1)}, s32[1,128]{1,0:T(1,128)}, u32[]{:S(2)}) copy-start(s32[1,128]{1,0:T(1,128)} %count_hbm.1) | copy-start | bytes 1540
  7.7 19.2 %slice-start = ((bf16[384,256]{1,0:T(8,128)(2,1)}), bf16[256,256]{1,0:T(8,128)(2,1)S(1)}, s32[]{:S(2)}) async-start(bf16[384,256]{1,0:T(8,128)(2,1)} %w1_ref.1), calls=%async_computation.3 | async-start | bytes 262144 | tf_op jit(solution)/shard_map/slice | solution.py:276
  7.7 19.3 %copy-start.1 = (bf16[256,128]{1,0:T(8,128)(2,1)S(1)}, bf16[256,128]{1,0:T(8,128)(2,1)}, u32[]{:S(2)}) copy-start(bf16[256,128]{1,0:T(8,128)(2,1)} %w2_ref.1) | copy-start | bytes 196612
  7.8 41.2 %all-to-all-start = ((bf16[128,32,256]{2,1,0:T(8,128)(2,1)}), bf16[128,32,256]{2,1,0:T(8,128)(2,1)S(1)}, u32[]{:S(2)}, u32[]{:S(2)}) async-start(bf16[128,32,256]{2,1,0:T(8,128)(2,1)} %bitcast.21), calls=%async_computation | async-start | bytes 4194304 | tf_op jit(solution)/shard_map/all_to_all | solution.py:435
  27.3 21.6 %copy-start = (bf16[384,256]{1,0:T(8,128)(2,1)S(1)}, bf16[384,256]{1,0:T(8,128)(2,1)}, u32[]{:S(2)}) copy-start(bf16[384,256]{1,0:T(8,128)(2,1)} %w1_ref.1) | copy-start | bytes 589828
  27.3 21.6 %copy-start.2 = (f32[256]{0:T(256)S(1)}, f32[256]{0:T(256)}, u32[]{:S(2)}) copy-start(f32[256]{0:T(256)} %param.16) | copy-start | bytes 3076
  63.4 37.9 %all-to-all-start.1 = ((bf16[128,72,128]{2,1,0:T(8,128)(2,1)}), bf16[128,72,128]{2,1,0:T(8,128)(2,1)}, u32[]{:S(2)}, u32[]{:S(2)}) async-start(bf16[128,72,128]{2,1,0:T(8,128)(2,1)} %get-tuple-element.21), calls=%async_computation.1 | async-start | bytes 4718592 | tf_op jit(solution)/shard_map/all_to_all | solution.py:446
  69.0 2.8 %copy-start.3 = (bf16[8192,256]{1,0:T(8,128)(2,1)S(1)}, bf16[8192,256]{1,0:T(8,128)(2,1)}, u32[]{:S(2)}) copy-start(bf16[8192,256]{1,0:T(8,128)(2,1)} %get-tuple-element.20) | copy-start | bytes 12582916
  71.8 3.0 %copy-start.8 = (bf16[2048,256]{1,0:T(8,128)(2,1)S(1)}, bf16[2048,256]{1,0:T(8,128)(2,1)}, u32[]{:S(2)}) copy-start(bf16[2048,256]{1,0:T(8,128)(2,1)} %get-tuple-element.16) | copy-start | bytes 3145732
  103.2 16.8 %all-to-all-start.2 = ((bf16[128,3,4,128]{3,2,1,0:T(4,128)(2,1)}), bf16[128,3,4,128]{3,2,1,0:T(4,128)(2,1)S(1)}, u32[]{:S(2)}, u32[]{:S(2)}) async-start(bf16[128,3,4,128]{3,2,1,0:T(4,128)(2,1)} %broadcast_in_dim.10), calls=%async_computation.2 | async-start | bytes 786432 | tf_op jit(solution)/shard_map/all_to_all | solution.py:458
  107.9 2.4 %copy-start.9 = (f32[2048,256]{1,0:T(8,128)S(1)}, f32[2048,256]{1,0:T(8,128)}, u32[]{:S(2)}) copy-start(f32[2048,256]{1,0:T(8,128)} %fusion.11) | copy-start | bytes 6291460

commit v7 on v6

--- a/solution.py
+++ b/solution.py
@@ -9,11 +9,11 @@
 
 AXES = ("phi", "eta")
 BLOCK = 4096
-GROUP = 16
+GROUP = 8
 PACK = 512
 SUPER = 4096
 CHUNK = 512
-ORDER = (3, 2, 1, 0)
+ORDER = (3, 2, 0, 1)
 PART = 256
 WINDOW = 256
 BF16 = jnp.bfloat16

time: 121 us -> 121 us (level)
  no operation moved by 1% of the time
where the time goes in v7:
time: 121 us
  matrix products  34.5 us (29%)
  waiting for transfers between devices  25.3 us (21%)
  Pallas kernels  22.5 us (19%)
  starting transfers between devices  21.7 us (18%)
  other arithmetic  8.48 us (7%)
  local copies, waits for them, and re-layouts  7.68 us (6%)
    dot_general x4, matrix products, dot(): return jnp.dot(a, b, preferred_element_type=F32)  34.5 us
    all_to_all x1, waiting for transfers between devices, local(): lax.all_to_all(outbound, AXES, split_axis=0, concat_axis=0, tiled=True)  14.7 us
    pallas_call x1, Pallas kernels, triplets(): pl.pallas_call(triplet_kernel, in_specs=[smem] * 3 + [vmem, hbm] + [vmem]...  14.5 us
    all_to_all x1, starting transfers between devices, local(): lax.all_to_all(outgoing, AXES, split_axis=0, concat_axis=0, tiled=True)  11.5 us
    all_to_all x1, waiting for transfers between devices, local(): lax.all_to_all(outgoing, AXES, split_axis=0, concat_axis=0, tiled=True)  7.53 us
    pallas_call x1, Pallas kernels, pack(): pl.pallas_call(pack_kernel, in_specs=[hbm] * 4, out_specs=[hbm] * 2, out_...  7.04 us
    sort x1, other arithmetic, local(): key = jnp.sort(trip_remote * rows + trip_local)  6.77 us
    all_to_all x1, starting transfers between devices, local(): lax.all_to_all(outbound, AXES, split_axis=0, concat_axis=0, tiled=True)  5.57 us
  transfers between devices with their start and end apart: 3, of which 3 were waited for; matrix products, arithmetic and copies ran while one was open for 39% of the time, Pallas kernels for 0%

profile of v7, /device:TPU:1, one launch (start us, length us, event | category | flops | bytes accessed | tf_op | source)
XLA Modules:
  0.0 121.0 jit_solution(16580803001183062210)
XLA Ops:
  0.6 7.0 %pack.1 = (bf16[2048,256]{1,0:T(8,128)(2,1)}, bf16[4096,256]{1,0:T(8,128)(2,1)}) custom-call(bf16[2048,128]{1,0:T(8,128)(2,1)} %edges_hbm.1, bf16[2048,128]{1,0:T(8,128)(2,1)} %cot_hbm.1, s32[32,128]{1,0:T(8,128)} %bitcast.23, s32[1,128]{1,0:T(1,128)} %count_hbm.1), custom_call_target="tpu_custom_call" | custom-call | flops 4294967296 | bytes 4194304 | tf_op jit(solution)/shard_map/pack/pallas_call | solution.py:354
  7.8 11.5 %all-to-all-start = ((bf16[128,32,256]{2,1,0:T(8,128)(2,1)}), bf16[128,32,256]{2,1,0:T(8,128)(2,1)S(1)}, u32[]{:S(2)}, u32[]{:S(2)}) async-start(bf16[128,32,256]{2,1,0:T(8,128)(2,1)} %bitcast.21), calls=%async_computation | async-start | bytes 4194304 | tf_op jit(solution)/shard_map/all_to_all | solution.py:435
  19.4 6.8 %sort.15 = (s32[8192]{0:T(1024)S(1)}, s32[8192]{0:T(1024)}) sort(s32[8192]{0:T(1024)S(1)} %multiply_add_fusion, s32[8192]{0:T(1024)S(1)} %iota.15), dimensions={0}, to_apply=%region_0.1 | sort | flops 106496 | bytes 131072 | tf_op jit(solution)/shard_map/order/jit(sort)/sort | solution.py:438
  26.2 0.2 slice_reduce_fusion.1
  27.0 0.1 copy.20
  27.1 0.1 add_reduce_fusion.most_ref
  27.3 14.1 %fusion.6.own_hbm = bf16[8192,256]{1,0:T(8,128)(2,1)} fusion(bf16[2048,256]{1,0:T(8,128)(2,1)} %get-tuple-element.16, s32[8192]{0:T(1024)S(1)} %get-tuple-element.34), kind=kOutput, calls=%fused_computation.9 | convolution fusion | flops 8608808960 | bytes 5275648 | tf_op jit(solution)/shard_map/own_rows/dot_general | solution.py:24
  41.4 7.5 %all-to-all-done = bf16[128,32,256]{2,1,0:T(8,128)(2,1)S(1)} async-done(((bf16[128,32,256]{2,1,0:T(8,128)(2,1)}), bf16[128,32,256]{2,1,0:T(8,128)(2,1)S(1)}, u32[]{:S(2)}, u32[]{:S(2)}) %all-to-all-start) | async-done | bytes 2097184 | tf_op jit(solution)/shard_map/all_to_all | solution.py:435
  48.9 14.5 %triplets.1 = (bf16[8192,256]{1,0:T(8,128)(2,1)}, bf16[8192,256]{1,0:T(8,128)(2,1)}, bf16[128,72,128]{2,1,0:T(8,128)(2,1)}, f32[1,256]{1,0:T(1,128)S(1)}) custom-call(s32[32]{0:T(128)S(1)} %get-tuple-element.29.base_ref, s32[32]{0:T(128)S(1)} %get-tuple-element.28.count_ref, s32[2]{0:T(128)S(1)} %add_reduce_fusion.most_ref, s32[32,1,256]{2,1,0:T(1,128)S(1)} %bitcast.17, ...), custom_call_target="tpu_custom_call" | custom-call | flops 9830400000 | bytes 20971520 | tf_op jit(solution)/shard_map/triplets/pallas_call | solution.py:248
  63.4 5.6 %all-to-all-start.1 = ((bf16[128,72,128]{2,1,0:T(8,128)(2,1)}), bf16[128,72,128]{2,1,0:T(8,128)(2,1)}, u32[]{:S(2)}, u32[]{:S(2)}) async-start(bf16[128,72,128]{2,1,0:T(8,128)(2,1)} %get-tuple-element.21), calls=%async_computation.1 | async-start | bytes 4718592 | tf_op jit(solution)/shard_map/all_to_all | solution.py:446
  69.0 1.9 %slice.36 = bf16[8192,128]{1,0:T(8,128)(2,1)S(1)} slice(bf16[8192,256]{1,0:T(8,128)(2,1)} %get-tuple-element.19), slice={[0:8192], [0:128]} | slice | bytes 4194304 | tf_op jit(solution)/shard_map/own_sums/slice | solution.py:449
  70.9 0.9 copy-done.3
  71.8 3.0 %fusion.7 = bf16[8192,128]{1,0:T(8,128)(2,1)S(1)} fusion(bf16[8192,256]{1,0:T(8,128)(2,1)S(1)} %copy-done.3, bf16[8192,256]{1,0:T(8,128)(2,1)} %get-tuple-element.19, bf16[384,256]{1,0:T(8,128)(2,1)S(1)} %copy-done), kind=kOutput, calls=%fused_computation.11 | convolution fusion | flops 540016640 | bytes 8454144 | tf_op jit(solution)/shard_map/own_sums/dot_general | solution.py:24
  74.8 11.7 %fusion.11 = f32[2048,256]{1,0:T(8,128)} fusion(bf16[8192,128]{1,0:T(8,128)(2,1)S(1)} %fusion.7, bf16[8192,128]{1,0:T(8,128)(2,1)S(1)} %slice.36, s32[8192]{0:T(1024)S(1)} %get-tuple-element.34, bf16[2048,256]{1,0:T(8,128)(2,1)S(1)} %copy-done.8), kind=kOutput, calls=%fused_computation.15 | convolution fusion | flops 8616148992 | bytes 7372800 | tf_op jit(solution)/shard_map/own_sums/dot_general | solution.py:24
  86.5 14.7 %all-to-all-done.1 = bf16[128,72,128]{2,1,0:T(8,128)(2,1)} async-done(((bf16[128,72,128]{2,1,0:T(8,128)(2,1)}), bf16[128,72,128]{2,1,0:T(8,128)(2,1)}, u32[]{:S(2)}, u32[]{:S(2)}) %all-to-all-start.1) | async-done | bytes 2359328 | tf_op jit(solution)/shard_map/all_to_all | solution.py:446
  101.3 1.1 slice_reduce_fusion
  102.4 0.9 broadcast_in_dim.10
  103.2 4.6 %all-to-all-start.2 = ((bf16[128,3,4,128]{3,2,1,0:T(4,128)(2,1)}), bf16[128,3,4,128]{3,2,1,0:T(4,128)(2,1)S(1)}, u32[]{:S(2)}, u32[]{:S(2)}) async-start(bf16[128,3,4,128]{3,2,1,0:T(4,128)(2,1)} %broadcast_in_dim.10), calls=%async_computation.2 | async-start | bytes 786432 | tf_op jit(solution)/shard_map/all_to_all | solution.py:458
  107.9 2.1 %fusion.22 = (bf16[128,32,128]{2,1,0:T(8,128)(2,1)S(1)}, bf16[128,32,128]{2,1,0:T(8,128)(2,1)S(1)}) fusion(bf16[128,72,128]{2,1,0:T(8,128)(2,1)} %all-to-all-done.1), kind=kLoop, calls=%fused_computation.59 | loop fusion | bytes 4194304 | tf_op jit(solution)/shard_map/far_sums/slice | solution.py:461
  109.9 0.3 pad_maximum_fusion
  110.3 5.7 %fusion.15 = bf16[2048,256]{1,0:T(8,128)(2,1)S(1)} fusion(f32[2048,256]{1,0:T(8,128)S(1)} %copy-done.9, bf16[4096,256]{1,0:T(8,128)(2,1)S(1)} %bitcast.22, s32[4096]{0:T(1024)S(1)} %broadcast_select_fusion), kind=kOutput, calls=%fused_computation.17 | convolution fusion | flops 4304404480 | bytes 5259264 | tf_op jit(solution)/shard_map/far_sums/dot_general | solution.py:24
  116.0 1.0 fusion.23
  117.0 3.0 %all-to-all-done.2.shared_ref = bf16[128,3,4,128]{3,2,1,0:T(4,128)(2,1)S(1)} async-done(((bf16[128,3,4,128]{3,2,1,0:T(4,128)(2,1)}), bf16[128,3,4,128]{3,2,1,0:T(4,128)(2,1)S(1)}, u32[]{:S(2)}, u32[]{:S(2)}) %all-to-all-start.2) | async-done | bytes 393248 | tf_op jit(solution)/shard_map/all_to_all | solution.py:458
  120.0 1.0 unpack.1
  (38 shorter events, 0.8 us)
Async XLA Ops:
  7.7 11.6 %copy-start.6 = (s32[1,128,32]{1,2,0:T(8,128)S(1)}, s32[1,128,32]{1,2,0:T(8,128)}, u32[]{:S(2)}) copy-start(s32[1,128,32]{1,2,0:T(8,128)} %param.11) | copy-start | bytes 49156
  7.7 11.7 %copy-start.4 = (s32[8192]{0:T(1024)S(1)}, s32[8192]{0:T(1024)}, u32[]{:S(2)}) copy-start(s32[8192]{0:T(1024)} %param.13) | copy-start | bytes 98308
  7.7 11.7 %copy-start.5 = (s32[8192]{0:T(1024)S(1)}, s32[8192]{0:T(1024)}, u32[]{:S(2)}) copy-start(s32[8192]{0:T(1024)} %param.14) | copy-start | bytes 98308
  7.7 18.8 %copy-start.7 = (s32[1,128]{1,0:T(1,128)S(1)}, s32[1,128]{1,0:T(1,128)}, u32[]{:S(2)}) copy-start(s32[1,128]{1,0:T(1,128)} %count_hbm.1) | copy-start | bytes 1540
  7.7 19.2 %slice-start = ((bf16[384,256]{1,0:T(8,128)(2,1)}), bf16[256,256]{1,0:T(8,128)(2,1)S(1)}, s32[]{:S(2)}) async-start(bf16[384,256]{1,0:T(8,128)(2,1)} %w1_ref.1), calls=%async_computation.3 | async-start | bytes 262144 | tf_op jit(solution)/shard_map/slice | solution.py:276
  7.7 19.3 %copy-start.1 = (bf16[256,128]{1,0:T(8,128)(2,1)S(1)}, bf16[256,128]{1,0:T(8,128)(2,1)}, u32[]{:S(2)}) copy-start(bf16[256,128]{1,0:T(8,128)(2,1)} %w2_ref.1) | copy-start | bytes 196612
  7.8 41.2 %all-to-all-start = ((bf16[128,32,256]{2,1,0:T(8,128)(2,1)}), bf16[128,32,256]{2,1,0:T(8,128)(2,1)S(1)}, u32[]{:S(2)}, u32[]{:S(2)}) async-start(bf16[128,32,256]{2,1,0:T(8,128)(2,1)} %bitcast.21), calls=%async_computation | async-start | bytes 4194304 | tf_op jit(solution)/shard_map/all_to_all | solution.py:435
  27.3 21.6 %copy-start = (bf16[384,256]{1,0:T(8,128)(2,1)S(1)}, bf16[384,256]{1,0:T(8,128)(2,1)}, u32[]{:S(2)}) copy-start(bf16[384,256]{1,0:T(8,128)(2,1)} %w1_ref.1) | copy-start | bytes 589828
  27.3 21.6 %copy-start.2 = (f32[256]{0:T(256)S(1)}, f32[256]{0:T(256)}, u32[]{:S(2)}) copy-start(f32[256]{0:T(256)} %param.16) | copy-start | bytes 3076
  63.4 37.9 %all-to-all-start.1 = ((bf16[128,72,128]{2,1,0:T(8,128)(2,1)}), bf16[128,72,128]{2,1,0:T(8,128)(2,1)}, u32[]{:S(2)}, u32[]{:S(2)}) async-start(bf16[128,72,128]{2,1,0:T(8,128)(2,1)} %get-tuple-element.21), calls=%async_computation.1 | async-start | bytes 4718592 | tf_op jit(solution)/shard_map/all_to_all | solution.py:446
  69.0 2.8 %copy-start.3 = (bf16[8192,256]{1,0:T(8,128)(2,1)S(1)}, bf16[8192,256]{1,0:T(8,128)(2,1)}, u32[]{:S(2)}) copy-start(bf16[8192,256]{1,0:T(8,128)(2,1)} %get-tuple-element.20) | copy-start | bytes 12582916
  71.8 3.0 %copy-start.8 = (bf16[2048,256]{1,0:T(8,128)(2,1)S(1)}, bf16[2048,256]{1,0:T(8,128)(2,1)}, u32[]{:S(2)}) copy-start(bf16[2048,256]{1,0:T(8,128)(2,1)} %get-tuple-element.16) | copy-start | bytes 3145732
  103.2 16.8 %all-to-all-start.2 = ((bf16[128,3,4,128]{3,2,1,0:T(4,128)(2,1)}), bf16[128,3,4,128]{3,2,1,0:T(4,128)(2,1)S(1)}, u32[]{:S(2)}, u32[]{:S(2)}) async-start(bf16[128,3,4,128]{3,2,1,0:T(4,128)(2,1)} %broadcast_in_dim.10), calls=%async_computation.2 | async-start | bytes 786432 | tf_op jit(solution)/shard_map/all_to_all | solution.py:458
  107.9 2.4 %copy-start.9 = (f32[2048,256]{1,0:T(8,128)S(1)}, f32[2048,256]{1,0:T(8,128)}, u32[]{:S(2)}) copy-start(f32[2048,256]{1,0:T(8,128)} %fusion.11) | copy-start | bytes 6291460
